TPU v7x, 32 devices: a whole 2x2x4 slice. The times are simulated.
32 devices in a mesh: dp: 16 (over z, x, core), shard: 2 (over y).
Axes of the slice: x: 2, y: 2, z: 4, core: 2. Of those that a mesh axis runs over, the one named last changes fastest.
Arguments:
- tokens: bfloat16 [32768, 768], P(('dp', 'shard')), may hold values from -2.5 to 2.5
- cotangent: bfloat16 [32768, 768], P(('dp', 'shard')), may hold values from -2.5 to 2.5
- master_qkv: float32 [768, 2304], P('shard'), may hold values from -0.21875 to 0.21875
- first_qkv: float32 [768, 2304], P('shard'), may hold values from -2.5 to 2.5
- second_qkv: float32 [768, 2304], P('shard'), may hold values from 0.25 to 4
- master_out: float32 [768, 768], P('shard'), may hold values from -0.875 to 0.875
- first_out: float32 [768, 768], P('shard'), may hold values from -2.5 to 2.5
- second_out: float32 [768, 768], P('shard'), may hold values from 0.01 to 0.16
- master_gate_up: float32 [768, 6144], P('shard'), may hold values from -0.21875 to 0.21875
- first_gate_up: float32 [768, 6144], P('shard'), may hold values from -2.5 to 2.5
- second_gate_up: float32 [768, 6144], P('shard'), may hold values from 0.02 to 0.32
- master_down: float32 [3072, 768], P('shard'), may hold values from -0.109375 to 0.109375
- first_down: float32 [3072, 768], P('shard'), may hold values from -2.5 to 2.5
- second_down: float32 [3072, 768], P('shard'), may hold values from 0.25 to 4
- norms: float32 [4, 768], replicated, may hold values from -2.5 to 2.5, as said below
- norm_first: float32 [4, 768], replicated, may hold values from -2.5 to 2.5
- norm_second: float32 [4, 768], replicated, may hold values from 0.25 to 4
Outputs:
- output: bfloat16 [32768, 768], P(('dp', 'shard'))
- input_grad: bfloat16 [32768, 768], P(('dp', 'shard'))
- new_qkv: bfloat16 [768, 2304], replicated
- new_out: bfloat16 [768, 768], replicated
- new_gate_up: bfloat16 [768, 6144], replicated
- new_down: bfloat16 [3072, 768], replicated
- next_first_qkv: float32 [768, 2304], P('shard')
- next_second_qkv: float32 [768, 2304], P('shard')
- next_first_out: float32 [768, 768], P('shard')
- next_second_out: float32 [768, 768], P('shard')
- next_first_gate_up: float32 [768, 6144], P('shard')
- next_second_gate_up: float32 [768, 6144], P('shard')
- next_first_down: float32 [3072, 768], P('shard')
- next_second_down: float32 [3072, 768], P('shard')
- new_norms: float32 [4, 768], replicated
- next_norm_first: float32 [4, 768], replicated
- next_norm_second: float32 [4, 768], replicated
Inputs may be any that keep to these rules, and one draw needn't show every extreme that they name: Rows 0 and 2 of norms are gains near 1, rows 1 and 3 biases.
All inputs are finite; a program needn't handle non-finite values.
Results may differ from a plain program's by a relative error of at most 0.018.
Values may be sent and summed in bfloat16 or wider, within the bound.
A program may use at most 320 MiB of HBM per device.

v0:
```python
import math

import jax
import jax.numpy as jnp
from jax import lax
from jax.sharding import PartitionSpec as P

HEADS = 12
HEAD_DIM = 64
STEP = 3


norm_eps = 1e-12
rope_base = 1000.0
learn_rate = 0.03
norm_rate = 0.3
decay_rate = 0.1
adam_eps = 1e-08
beta_first = 0.5
beta_second = 0.5


def rope_tables(length, head_width):
    half_width = head_width // 2
    frequency = rope_base ** (-(jnp.arange(half_width, dtype=jnp.float32) * (2.0 / head_width)))
    angles = jnp.arange(length, dtype=jnp.float32)[:, None] * frequency[None, :]
    angles = jnp.concatenate([angles, angles], axis=1)
    return (jnp.cos(angles), jnp.sin(angles))


def turn_half(vectors):
    half_width = vectors.shape[-1] // 2
    return jnp.concatenate([-vectors[..., half_width:], vectors[..., :half_width]], axis=-1)


def rotate(vectors, cosine, sine_table):
    return vectors * cosine[:, None, :] + turn_half(vectors) * sine_table[:, None, :]


def unrotate(grads, cosine, sine_table):
    return grads * cosine[:, None, :] - turn_half(grads * sine_table[:, None, :])


def norm_forward(values, gain_row, bias_row):
    centred = values - jnp.mean(values, axis=1, keepdims=True)
    inverse = lax.rsqrt(jnp.mean(centred * centred, axis=1, keepdims=True) + norm_eps)
    normed = centred * inverse
    return (normed * gain_row + bias_row, normed, inverse)


def norm_backward(grad_rows, normed, inverse, gain_row):
    scaled = grad_rows * gain_row
    centred = (
        scaled
        - jnp.mean(scaled, axis=1, keepdims=True)
        - normed * jnp.mean(scaled * normed, axis=1, keepdims=True)
    )
    return (centred * inverse, jnp.sum(grad_rows * normed, axis=0), jnp.sum(grad_rows, axis=0))


def outer_sum(left, right):
    return lax.dot_general(
        left, right, (((0,), (0,)), ((), ())), preferred_element_type=jnp.float32
    )


def back_dot(grad_rows, weight):
    return lax.dot_general(
        grad_rows, weight, (((1,), (1,)), ((), ())), preferred_element_type=jnp.float32
    )


def attend_forward(queries, key_rows, value_rows, block_rows):
    length, head_count, head_width = queries.shape
    count = length // block_rows

    def one_block(query_block):
        scores = jnp.einsum(
            "qhd,khd->hqk", query_block, key_rows, preferred_element_type=jnp.float32
        )
        highest = jnp.max(scores, axis=2, keepdims=True)
        expanded = jnp.exp(scores - highest)
        totals = jnp.sum(expanded, axis=2, keepdims=True)
        weights_soft = (expanded / totals).astype(jnp.bfloat16)
        mixed_block = jnp.einsum(
            "hqk,khd->qhd", weights_soft, value_rows, preferred_element_type=jnp.float32
        )
        return (mixed_block.astype(jnp.bfloat16), highest[..., 0] + jnp.log(totals[..., 0]))

    mixed_rows, logsum = lax.map(
        one_block, queries.reshape(count, block_rows, head_count, head_width)
    )
    return (mixed_rows.reshape(length, head_count * head_width), logsum)


def attend_backward(queries, key_rows, value_rows, grad_mixed, logsum, block_rows):
    length, head_count, head_width = queries.shape
    count = length // block_rows

    def one_block(carry, pieces):
        key_grad, value_grad = carry
        query_block, grad_block, logsum_block = pieces
        scores = jnp.einsum(
            "qhd,khd->hqk", query_block, key_rows, preferred_element_type=jnp.float32
        )
        weights_soft = jnp.exp(scores - logsum_block[:, :, None])
        value_grad = value_grad + jnp.einsum(
            "hqk,qhd->khd",
            weights_soft.astype(jnp.bfloat16),
            grad_block,
            preferred_element_type=jnp.float32,
        )
        weight_grad = jnp.einsum(
            "qhd,khd->hqk", grad_block, value_rows, preferred_element_type=jnp.float32
        )
        centre = jnp.sum(weights_soft * weight_grad, axis=2, keepdims=True)
        score_grad = (weights_soft * (weight_grad - centre)).astype(jnp.bfloat16)
        query_grad = jnp.einsum(
            "hqk,khd->qhd", score_grad, key_rows, preferred_element_type=jnp.float32
        )
        key_grad = key_grad + jnp.einsum(
            "hqk,qhd->khd", score_grad, query_block, preferred_element_type=jnp.float32
        )
        return ((key_grad, value_grad), query_grad)

    zeros_acc = jnp.zeros((length, head_count, head_width), jnp.float32)
    shaped = (
        queries.reshape(count, block_rows, head_count, head_width),
        grad_mixed.reshape(count, block_rows, head_count, head_width),
        logsum,
    )
    (key_grad, value_grad), query_grad = lax.scan(one_block, (zeros_acc, zeros_acc), shaped)
    return (query_grad.reshape(length, head_count, head_width), key_grad, value_grad)


def adam_update(weight, first_moment, second_moment, gradient, rate, decay_on):
    first_new = beta_first * first_moment + (1.0 - beta_first) * gradient
    second_new = beta_second * second_moment + (1.0 - beta_second) * gradient * gradient
    fix_first = 1.0 - beta_first**STEP
    fix_second = 1.0 - beta_second**STEP
    direction = first_new / fix_first / (jnp.sqrt(second_new / fix_second) + adam_eps)
    return (weight - rate * (direction + decay_on * weight), first_new, second_new)


def shards(
    tokens,
    cotangent,
    master_qkv,
    first_qkv,
    second_qkv,
    master_out,
    first_out,
    second_out,
    master_gate_up,
    first_gate_up,
    second_gate_up,
    master_down,
    first_down,
    second_down,
    norms,
    norm_first,
    norm_second,
):
    length = tokens.shape[0]
    block_rows = min(512, length)
    weight_qkv, weight_out, weight_gate_up, weight_down = (
        lax.all_gather(master_qkv.astype(jnp.bfloat16), "shard", axis=0, tiled=True),
        lax.all_gather(master_out.astype(jnp.bfloat16), "shard", axis=0, tiled=True),
        lax.all_gather(master_gate_up.astype(jnp.bfloat16), "shard", axis=0, tiled=True),
        lax.all_gather(master_down.astype(jnp.bfloat16), "shard", axis=0, tiled=True),
    )
    cosine, sine_table = rope_tables(length, HEAD_DIM)
    query_scale = 1.0 / math.sqrt(HEAD_DIM)
    joined_rows = jnp.dot(tokens, weight_qkv, preferred_element_type=jnp.float32).reshape(
        length, 3, HEADS, HEAD_DIM
    )
    queries = (rotate(joined_rows[:, 0], cosine, sine_table) * query_scale).astype(jnp.bfloat16)
    key_rows = rotate(joined_rows[:, 1], cosine, sine_table).astype(jnp.bfloat16)
    value_rows = joined_rows[:, 2].astype(jnp.bfloat16)
    mixed_rows, logsum = attend_forward(queries, key_rows, value_rows, block_rows)
    first_sum = tokens.astype(jnp.float32) + jnp.dot(
        mixed_rows, weight_out, preferred_element_type=jnp.float32
    )
    hidden, normed_one, inverse_one = norm_forward(first_sum, norms[0], norms[1])
    hidden_low = hidden.astype(jnp.bfloat16)
    gate_up = jnp.dot(hidden_low, weight_gate_up, preferred_element_type=jnp.float32)
    split_at = gate_up.shape[1] // 2
    gate_part = gate_up[:, :split_at]
    up_part = gate_up[:, split_at:]
    sigmoid = jax.nn.sigmoid(gate_part)
    swished = gate_part * sigmoid
    inner_rows = (swished * up_part).astype(jnp.bfloat16)
    second_sum = hidden + jnp.dot(inner_rows, weight_down, preferred_element_type=jnp.float32)
    output, normed_two, inverse_two = norm_forward(second_sum, norms[2], norms[3])
    grad_second, gain_two, bias_two = norm_backward(
        cotangent.astype(jnp.float32), normed_two, inverse_two, norms[2]
    )
    branch_two_grad = grad_second.astype(jnp.bfloat16)
    down_grad = outer_sum(inner_rows, branch_two_grad)
    inner_grad = back_dot(branch_two_grad, weight_down)
    gate_grad = inner_grad * up_part * sigmoid * (1.0 + gate_part * (1.0 - sigmoid))
    up_grad = inner_grad * swished
    gate_up_back = jnp.concatenate([gate_grad, up_grad], axis=1).astype(jnp.bfloat16)
    gate_up_grad = outer_sum(hidden_low, gate_up_back)
    hidden_grad = grad_second + back_dot(gate_up_back, weight_gate_up)
    grad_first, gain_one, bias_one = norm_backward(hidden_grad, normed_one, inverse_one, norms[0])
    branch_one_grad = grad_first.astype(jnp.bfloat16)
    out_grad = outer_sum(mixed_rows, branch_one_grad)
    mixed_grad = (
        back_dot(branch_one_grad, weight_out).astype(jnp.bfloat16).reshape(length, HEADS, HEAD_DIM)
    )
    query_grad, key_grad, value_grad = attend_backward(
        queries, key_rows, value_rows, mixed_grad, logsum, block_rows
    )
    joined_grad = jnp.stack(
        [
            unrotate(query_grad, cosine, sine_table) * query_scale,
            unrotate(key_grad, cosine, sine_table),
            value_grad,
        ],
        axis=1,
    )
    joined_grad = joined_grad.reshape(length, 3 * HEADS * HEAD_DIM).astype(jnp.bfloat16)
    qkv_grad = outer_sum(tokens, joined_grad)
    input_grad = (grad_first + back_dot(joined_grad, weight_qkv)).astype(jnp.bfloat16)
    qkv_part, out_part, gate_up_part, down_part = (
        lax.psum_scatter(
            qkv_grad.astype(jnp.bfloat16), "shard", scatter_dimension=0, tiled=True
        ).astype(jnp.float32),
        lax.psum_scatter(
            out_grad.astype(jnp.bfloat16), "shard", scatter_dimension=0, tiled=True
        ).astype(jnp.float32),
        lax.psum_scatter(
            gate_up_grad.astype(jnp.bfloat16), "shard", scatter_dimension=0, tiled=True
        ).astype(jnp.float32),
        lax.psum_scatter(
            down_grad.astype(jnp.bfloat16), "shard", scatter_dimension=0, tiled=True
        ).astype(jnp.float32),
    )
    qkv_total, out_total, gate_up_total, down_total = (
        lax.psum(qkv_part.astype(jnp.bfloat16), "dp").astype(jnp.float32),
        lax.psum(out_part.astype(jnp.bfloat16), "dp").astype(jnp.float32),
        lax.psum(gate_up_part.astype(jnp.bfloat16), "dp").astype(jnp.float32),
        lax.psum(down_part.astype(jnp.bfloat16), "dp").astype(jnp.float32),
    )
    norm_total = lax.psum(jnp.stack([gain_one, bias_one, gain_two, bias_two]), ("dp", "shard"))
    scale_grad = 1.0 / math.sqrt(length * lax.axis_size("dp") * lax.axis_size("shard"))
    upd_qkv, first_qkv_new, second_qkv_new = adam_update(
        master_qkv, first_qkv, second_qkv, qkv_total * scale_grad, learn_rate, decay_rate
    )
    upd_out, first_out_new, second_out_new = adam_update(
        master_out, first_out, second_out, out_total * scale_grad, learn_rate, decay_rate
    )
    upd_gate_up, first_gate_up_new, second_gate_up_new = adam_update(
        master_gate_up,
        first_gate_up,
        second_gate_up,
        gate_up_total * scale_grad,
        learn_rate,
        decay_rate,
    )
    upd_down, first_down_new, second_down_new = adam_update(
        master_down, first_down, second_down, down_total * scale_grad, learn_rate, decay_rate
    )
    upd_norms, norm_first_new, norm_second_new = adam_update(
        norms, norm_first, norm_second, norm_total * scale_grad, norm_rate, 0.0
    )
    full_qkv, full_out, full_gate_up, full_down = (
        lax.all_gather(upd_qkv.astype(jnp.bfloat16), "shard", axis=0, tiled=True),
        lax.all_gather(upd_out.astype(jnp.bfloat16), "shard", axis=0, tiled=True),
        lax.all_gather(upd_gate_up.astype(jnp.bfloat16), "shard", axis=0, tiled=True),
        lax.all_gather(upd_down.astype(jnp.bfloat16), "shard", axis=0, tiled=True),
    )
    return (
        output.astype(jnp.bfloat16),
        input_grad,
        full_qkv,
        full_out,
        full_gate_up,
        full_down,
        first_qkv_new,
        second_qkv_new,
        first_out_new,
        second_out_new,
        first_gate_up_new,
        second_gate_up_new,
        first_down_new,
        second_down_new,
        upd_norms,
        norm_first_new,
        norm_second_new,
    )


def solution(mesh):
    return jax.shard_map(
        shards,
        mesh=mesh,
        in_specs=(
            P(("dp", "shard"), None),
            P(("dp", "shard"), None),
            P("shard", None),
            P("shard", None),
            P("shard", None),
            P("shard", None),
            P("shard", None),
            P("shard", None),
            P("shard", None),
            P("shard", None),
            P("shard", None),
            P("shard", None),
            P("shard", None),
            P("shard", None),
            P(),
            P(),
            P(),
        ),
        out_specs=(
            P(("dp", "shard"), None),
            P(("dp", "shard"), None),
            P(),
            P(),
            P(),
            P(),
            P("shard", None),
            P("shard", None),
            P("shard", None),
            P("shard", None),
            P("shard", None),
            P("shard", None),
            P("shard", None),
            P("shard", None),
            P(),
            P(),
            P(),
        ),
        check_vma=False,
    )
```

profile of v0, /device:TPU:0, one launch (start us, length us, event | category | flops | bytes accessed | tf_op | source)
XLA Modules:
  0.0 1325.5 jit_solution(369332038078282197)
XLA Ops:
  33.1 29.8 %all-gather.9.cloned.1.call-done = bf16[768,2304]{1,0:T(8,128)(2,1)} async-done(((bf16[384,2304]{1,0:T(8,128)(2,1)}), bf16[768,2304]{1,0:T(8,128)(2,1)}) %all-gather.9.cloned.1.call-update) | async-done | bytes 3538960 | tf_op jit(solution)/shard_map/all_gather | solution.py:167
  96.6 68.0 %while.27 = (s32[]{:T(128)}, bf16[2,512,12,64]{1,3,2,0:T(8,128)(2,1)}, f32[2,12,512]{2,1,0:T(8,128)S(1)}, bf16[2,512,12,64]{1,3,2,0:T(8,128)(2,1)S(1)}, bf16[102...) while((s32[]{:T(128)}, bf16[2,512,12,64]{1,3,2,0:T(8,128)(2,1)}, ...), condition=%wide.region_3.4_spmd, body=%wide.region_0.3_spmd.sunk | while | flops 1648748544 | bytes 86729328 | solution.py:90
  96.6 13.1 fusion.133
  109.7 11.2 fusion.134
  120.9 11.3 fusion.135
  142.3 11.0 fusion.134
  153.4 11.3 fusion.135
  175.1 33.0 %all-gather.13.cloned.1.call-done = bf16[768,6144]{1,0:T(8,128)(2,1)} async-done(((bf16[384,6144]{1,0:T(8,128)(2,1)}), bf16[768,6144]{1,0:T(8,128)(2,1)}) %all-gather.13.cloned.1.call-update) | async-done | bytes 9437200 | tf_op jit(solution)/shard_map/all_gather | solution.py:169
  208.1 19.7 %fusion.77 = f32[1024,6144]{1,0:T(8,128)} fusion(bf16[768,6144]{1,0:T(8,128)(2,1)} %all-gather.13.cloned.1.call-done, f32[1024,768]{0,1:T(8,128)} %copy-done.5, f32[768]{0:T(1024)S(1)} %copy-done.35, f32[768]{0:T(1024)S(1)} %copy-done.31, f32[1024]{0:T(1024)S(1)} %add_rsqrt_fusion.1, f32[1024]{0:T(1024)S(1)} %broadcast_multiply_fusion.8), kind=kOutput, calls=%fused_computation.158 | convolution fusion | flops 9667608576 | bytes 37763072 | tf_op jit(solution)/shard_map/dot_general | solution.py:186
  227.8 12.7 multiply_convert_fusion.3
  240.5 32.3 %all-gather.15.cloned.1.call-done = bf16[3072,768]{1,0:T(8,128)(2,1)} async-done(((bf16[1536,768]{1,0:T(8,128)(2,1)}), bf16[3072,768]{1,0:T(8,128)(2,1)}) %all-gather.15.cloned.1.call-update) | async-done | bytes 4718608 | tf_op jit(solution)/shard_map/all_gather | solution.py:170
  288.1 21.8 %multiply_convert_fusion.2 = (bf16[1024,3072]{1,0:T(8,128)(2,1)}, bf16[1024,3072]{1,0:T(8,128)(2,1)}) fusion(f32[1024,6144]{1,0:T(8,128)} %fusion.77, bf16[3072,768]{1,0:T(8,128)(2,1)} %all-gather.15.cloned.1.call-done, f32[1024]{0:T(1024)S(1)} %broadcast_multiply_fusion.5, f32[1024]{0:T(1024)S(1)} %add_rsqrt_fusion, f32[1024,768]{0,1:T(8,128)} %copy-done.9, ...), kind=kOutput, calls=%fused_computation.38 | convolution fusion | flops 4879810560 | bytes 47205376 | tf_op jit(solution)/shard_map/dot_general | solution.py:68
  309.9 20.1 %multiply_reduce_fusion.1 = (f32[768]{0:T(1024)}, f32[1024]{0:T(1024)S(1)}, f32[1024]{0:T(1024)S(1)}, f32[768]{0:T(1024)}, f32[1024,768]{0,1:T(8,128)}) fusion(f32[1024,768]{0,1:T(8,128)} %copy-done.5, f32[1024]{0:T(1024)S(1)} %add_rsqrt_fusion.1, f32[1024]{0:T(1024)S(1)} %broadcast_multiply_fusion.8, f32[768]{0:T(1024)S(1)} %copy-done.31, ...), kind=kOutput, calls=%fused_computation.89 | convolution fusion | flops 9702993920 | bytes 33075200 | tf_op jit(solution)/shard_map/dot_general | solution.py:68
  347.4 223.7 %while.28 = (s32[]{:T(128)}, f32[1024,12,64]{0,2,1:T(8,128)}, f32[1024,12,64]{0,2,1:T(8,128)}, f32[2,512,12,64]{1,0,3,2:T(2,128)}, bf16[2,512,12,64]{1,3,2,0:T(8...) while((s32[]{:T(128)}, f32[1024,12,64]{0,2,1:T(8,128)}, ...), condition=%wide.region_14.15_spmd.clone, body=%wide.region_12.14_spmd.clone.sunk | while | flops 4086294528 | bytes 236111088 | solution.py:132
  358.0 16.5 %multiply_reduce_fusion.7 = (f32[12,512]{1,0:T(8,128)S(1)}, f32[12,512,1024]{2,1,0:T(8,128)}) fusion(f32[12,512,1024]{2,1,0:T(8,128)} %fusion.145, f32[12,512]{1,0:T(8,128)S(1)} %dynamic-slice_bitcast_fusion.2, bf16[1024,12,64]{0,2,1:T(8,128)(2,1)} %get-tuple-element.467, bf16[2,512,12,64]{1,3,2,0:T(8,128)(2,1)} %get-tuple-element.466, ...), kind=kOutput, calls=%fused_computation.13.clone.1 | convolution fusion | flops 824174592 | bytes 52740608 | tf_op jit(solution)/shard_map/while/body/eval_jaxpr/qhd,khd->hqk/dot_general | solution.py:113
  374.4 21.4 %multiply_convert_fusion.5 = bf16[12,512,1024]{2,1,0:T(8,128)(2,1)} fusion(f32[12,512,1024]{2,1,0:T(8,128)} %get-tuple-element.414, f32[12,512,1024]{2,1,0:T(8,128)} %fusion.145, f32[12,512]{1,0:T(8,128)S(1)} %get-tuple-element.415, f32[12,512]{1,0:T(8,128)S(1)} %dynamic-slice_bitcast_fusion.2), kind=kLoop, calls=%fused_computation.12.clone.1 | loop fusion | flops 25165824 | bytes 62963712 | tf_op jit(solution)/shard_map/while/body/eval_jaxpr/convert_element_type | solution.py:117
  408.5 28.7 %dynamic_update_slice.20 = f32[2,512,12,64]{1,0,3,2:T(2,128)} dynamic-update-slice(f32[2,512,12,64]{1,0,3,2:T(2,128)} %get-tuple-element.451, f32[1,512,12,64]{1,0,3,2:T(1,128)S(1)} %copy.113, s32[]{:T(128)} %get-tuple-element.448, s32[]{:T(128)} %constant.40.clone.1..sunk, s32[]{:T(128)} %constant.40.clone.1..sunk, s32[]{:T(128)} %constant.40.clone.1..sunk) | dynamic-update-slice | bytes 3145732 | tf_op jit(solution)/shard_map/while/body/jit(dynamic_update_index_in_dim)/dynamic_update_slice | solution.py:132
  446.1 12.4 bitcast_add_fusion.5
  468.6 16.5 %multiply_reduce_fusion.7 = (f32[12,512]{1,0:T(8,128)S(1)}, f32[12,512,1024]{2,1,0:T(8,128)}) fusion(f32[12,512,1024]{2,1,0:T(8,128)} %fusion.145, f32[12,512]{1,0:T(8,128)S(1)} %dynamic-slice_bitcast_fusion.2, bf16[1024,12,64]{0,2,1:T(8,128)(2,1)} %get-tuple-element.467, bf16[2,512,12,64]{1,3,2,0:T(8,128)(2,1)} %get-tuple-element.466, ...), kind=kOutput, calls=%fused_computation.13.clone.1 | convolution fusion | flops 824174592 | bytes 52740608 | tf_op jit(solution)/shard_map/while/body/eval_jaxpr/qhd,khd->hqk/dot_general | solution.py:113
  485.1 21.4 %multiply_convert_fusion.5 = bf16[12,512,1024]{2,1,0:T(8,128)(2,1)} fusion(f32[12,512,1024]{2,1,0:T(8,128)} %get-tuple-element.414, f32[12,512,1024]{2,1,0:T(8,128)} %fusion.145, f32[12,512]{1,0:T(8,128)S(1)} %get-tuple-element.415, f32[12,512]{1,0:T(8,128)S(1)} %dynamic-slice_bitcast_fusion.2), kind=kLoop, calls=%fused_computation.12.clone.1 | loop fusion | flops 25165824 | bytes 62963712 | tf_op jit(solution)/shard_map/while/body/eval_jaxpr/convert_element_type | solution.py:117
  519.2 28.7 %dynamic_update_slice.20 = f32[2,512,12,64]{1,0,3,2:T(2,128)} dynamic-update-slice(f32[2,512,12,64]{1,0,3,2:T(2,128)} %get-tuple-element.451, f32[1,512,12,64]{1,0,3,2:T(1,128)S(1)} %copy.113, s32[]{:T(128)} %get-tuple-element.448, s32[]{:T(128)} %constant.40.clone.1..sunk, s32[]{:T(128)} %constant.40.clone.1..sunk, s32[]{:T(128)} %constant.40.clone.1..sunk) | dynamic-update-slice | bytes 3145732 | tf_op jit(solution)/shard_map/while/body/jit(dynamic_update_index_in_dim)/dynamic_update_slice | solution.py:132
  557.7 13.3 %bitcast_add_fusion.5 = f32[1024,12,64]{0,2,1:T(8,128)} fusion(f32[1024,12,64]{0,2,1:T(8,128)} %get-tuple-element.450, f32[12,512,1024]{2,1,0:T(8,128)} %fusion.145, f32[12,512]{1,0:T(8,128)S(1)} %dynamic-slice_bitcast_fusion.2, pred[]{:T(512)S(6)} %compare.3, bf16[2,512,12,64]{1,3,2,0:T(8,128)(2,1)S(1)} %copy-done.4, s32[]{:T(128)} %get-tuple-element.448), kind=kOutput, calls=%fused_computation.18.clone.1 | convolution fusion | flops 819462144 | bytes 32276484 | tf_op jit(solution)/shard_map/while/body/eval_jaxpr/hqk,qhd->khd/dot_general | solution.py:107
  619.2 15.9 %convolution_convert_fusion = bf16[768,6144]{1,0:T(8,128)(2,1)} fusion(bf16[1024,3072]{1,0:T(8,128)(2,1)} %get-tuple-element.290, bf16[1024,3072]{1,0:T(8,128)(2,1)} %get-tuple-element.289, f32[1024,768]{0,1:T(8,128)S(1)} %copy-done.6, f32[768]{0:T(1024)S(1)} %copy-done.36, f32[768]{0:T(1024)S(1)} %copy-done.32, f32[1024]{0:T(1024)S(1)} %copy-done.34, ...), kind=kOutput, calls=%fused_computation.46 | convolution fusion | flops 9697492992 | bytes 25180160 | tf_op jit(solution)/shard_map/dot_general | solution.py:62
  635.2 13.9 %reduce-scatter.13.cloned.1.call-done = bf16[384,2304]{1,0:T(8,128)(2,1)} async-done(((bf16[768,2304]{1,0:T(8,128)(2,1)}), bf16[384,2304]{1,0:T(8,128)(2,1)}) %reduce-scatter.13.cloned.1.call-update) | async-done | bytes 1769488
  653.0 20.7 %reduce-scatter.7.cloned.1.call-done = bf16[384,768]{1,0:T(8,128)(2,1)} async-done(((bf16[768,768]{1,0:T(8,128)(2,1)}), bf16[384,768]{1,0:T(8,128)(2,1)}) %reduce-scatter.7.cloned.1.call-update) | async-done | bytes 589840 | tf_op jit(solution)/shard_map/reduce_scatter | solution.py:230
  673.7 62.9 %reduce-scatter.11.cloned.1.call-done = bf16[1536,768]{1,0:T(8,128)(2,1)} async-done(((bf16[3072,768]{1,0:T(8,128)(2,1)}), bf16[1536,768]{1,0:T(8,128)(2,1)}) %reduce-scatter.11.cloned.1.call-update) | async-done | bytes 2359312 | tf_op jit(solution)/shard_map/reduce_scatter | solution.py:236
  736.6 113.6 %reduce-scatter.9.cloned.1.call-done = bf16[384,6144]{1,0:T(8,128)(2,1)} async-done(((bf16[768,6144]{1,0:T(8,128)(2,1)}), bf16[384,6144]{1,0:T(8,128)(2,1)}) %reduce-scatter.9.cloned.1.call-update) | async-done | bytes 4718608 | tf_op jit(solution)/shard_map/reduce_scatter | solution.py:233
  866.5 174.8 %all-reduce.3.cloned.1.call-done = (bf16[384,2304]{0,1:T(8,128)(2,1)}, bf16[384,768]{1,0:T(8,128)(2,1)}, bf16[384,6144]{1,0:T(8,128)(2,1)}, bf16[1536,768]{1,0:T(8,128)(2,1)}) async-done(((bf16[384,2304]{0,1:T(8,128)(2,1)}, bf16[384,768]{1,0:T(8,128)(2,1)}, bf16[384,6144]{1,0:T(8,128)(2,1)}, bf16[1536,768]{1,0:T(8,128)(2,1)}), (bf16[384,2304]{0,1:T(8,128)(2,1)}, bf16[384,768]{1,0:T(8,128)(2,1)}, ...) | async-done | bytes 9437200 | tf_op jit(solution)/shard_map/psum | solution.py:241
  1063.3 21.9 %subtract_convert_fusion = (bf16[384,6144]{1,0:T(8,128)(2,1)}, f32[384,6144]{1,0:T(8,128)}, f32[384,6144]{1,0:T(8,128)}) fusion(f32[384,6144]{1,0:T(8,128)} %param.29, bf16[384,6144]{1,0:T(8,128)(2,1)} %get-tuple-element.268, f32[384,6144]{1,0:T(8,128)} %param.30, f32[384,6144]{1,0:T(8,128)} %param.31), kind=kLoop, calls=%fused_computation.48 | loop fusion | flops 40108032 | bytes 56623104 | tf_op jit(solution)/shard_map/convert_element_type | solution.py:271
  1102.9 40.6 %psum.39 = f32[4,768]{1,0:T(4,128)} all-reduce(f32[4,768]{1,0:T(4,128)S(1)} %pad_maximum_fusion.8), channel_id=1, replica_groups=mesh['dp'=16,'shard'=2] {'dp','shard'}, use_global_device_ids=true, to_apply=%region_27.28 | all-reduce | flops 3072 | bytes 24576 | tf_op jit(solution)/shard_map/psum | solution.py:246
  1158.9 25.1 %all-gather.23.cloned.1.call-done = bf16[3072,768]{1,0:T(8,128)(2,1)} async-done(((bf16[1536,768]{1,0:T(8,128)(2,1)}), bf16[3072,768]{1,0:T(8,128)(2,1)}) %all-gather.23.cloned.1.call-update) | async-done | bytes 4718608 | tf_op jit(solution)/shard_map/all_gather | solution.py:272
  1183.9 120.2 %all-gather.21.cloned.1.call-done = bf16[768,6144]{1,0:T(8,128)(2,1)} async-done(((bf16[384,6144]{1,0:T(8,128)(2,1)}), bf16[768,6144]{1,0:T(8,128)(2,1)}) %all-gather.21.cloned.1.call-update) | async-done | bytes 9437200 | tf_op jit(solution)/shard_map/all_gather | solution.py:271
  (239 shorter events, 314.4 us)
Async XLA Ops:
  7.2 55.8 %all-gather.9.cloned.1.call-start = ((), (), s32[]{:S(2)}) async-start(), calls=%async_computation.4 | async-start | bytes 5308416 | tf_op jit(solution)/shard_map/all_gather | solution.py:167
  10.7 158.5 %all-gather.11.cloned.1.call-start = ((), (), s32[]{:S(2)}) async-start(), calls=%async_computation.5 | async-start | bytes 1769472 | tf_op jit(solution)/shard_map/all_gather | solution.py:168
  11.7 196.4 %all-gather.13.cloned.1.call-start = ((), (), s32[]{:S(2)}) async-start(), calls=%async_computation.6 | async-start | bytes 14155776 | tf_op jit(solution)/shard_map/all_gather | solution.py:169
  18.3 254.4 %all-gather.15.cloned.1.call-start = ((), (), s32[]{:S(2)}) async-start(), calls=%async_computation.7 | async-start | bytes 7077888 | tf_op jit(solution)/shard_map/all_gather | solution.py:170
  22.9 626.2 %reduce-scatter.13.cloned.1.call-start = ((), (), s32[]{:S(2)}) async-start(), calls=%async_computation.15 | async-start | bytes 5308416
  24.8 67.6 %copy-start.18 = (f32[1024,64]{0,1:T(8,128)}, f32[1024,64]{0,1:T(8,128)S(1)}, u32[]{:S(2)}) copy-start(f32[1024,64]{0,1:T(8,128)S(1)} %get-tuple-element.305) | copy-start | bytes 786436
  109.7 11.2 copy-start.3
  142.3 11.0 copy-start.3
  173.0 35.0 %copy-start.31 = (f32[768]{0:T(1024)S(1)}, f32[768]{0:T(1024)}, u32[]{:S(2)}) copy-start(f32[768]{0:T(1024)} %get-tuple-element.234) | copy-start | bytes 9220
  173.1 35.0 %copy-start.35 = (f32[768]{0:T(1024)S(1)}, f32[768]{0:T(1024)}, u32[]{:S(2)}) copy-start(f32[768]{0:T(1024)} %get-tuple-element.233) | copy-start | bytes 9220
  173.1 157.0 %copy-start.29 = (f32[1024]{0:T(1024)}, f32[1024]{0:T(1024)S(1)}, u32[]{:S(2)}) copy-start(f32[1024]{0:T(1024)S(1)} %broadcast_multiply_fusion.8) | copy-start | bytes 12292
  175.1 154.9 %copy-start.33 = (f32[1024]{0:T(1024)}, f32[1024]{0:T(1024)S(1)}, u32[]{:S(2)}) copy-start(f32[1024]{0:T(1024)S(1)} %add_rsqrt_fusion.1) | copy-start | bytes 12292
  282.2 27.7 %copy-start.38 = (f32[1024]{0:T(1024)}, f32[1024]{0:T(1024)S(1)}, u32[]{:S(2)}) copy-start(f32[1024]{0:T(1024)S(1)} %broadcast_multiply_fusion.7) | copy-start | bytes 12292
  282.6 27.3 %copy-start.45 = (f32[1024]{0:T(1024)}, f32[1024]{0:T(1024)S(1)}, u32[]{:S(2)}) copy-start(f32[1024]{0:T(1024)S(1)} %add_rsqrt_fusion) | copy-start | bytes 12292
  288.1 21.8 %copy-start.48 = (f32[1024]{0:T(1024)}, f32[1024]{0:T(1024)S(1)}, u32[]{:S(2)}) copy-start(f32[1024]{0:T(1024)S(1)} %broadcast_multiply_fusion.5) | copy-start | bytes 12292
  288.1 21.8 %copy-start.50 = (f32[1024]{0:T(1024)}, f32[1024]{0:T(1024)S(1)}, u32[]{:S(2)}) copy-start(f32[1024]{0:T(1024)S(1)} %broadcast_multiply_fusion.6) | copy-start | bytes 12292
  347.8 10.2 copy-start.1
  446.1 12.4 copy-start.2
  458.5 10.1 copy-start.1
  557.7 13.3 %copy-start.2 = (bf16[2,512,12,64]{1,3,2,0:T(8,128)(2,1)S(1)}, bf16[2,512,12,64]{1,3,2,0:T(8,128)(2,1)}, u32[]{:S(2)}) copy-start(bf16[2,512,12,64]{1,3,2,0:T(8,128)(2,1)} %copy-done.1) | copy-start | bytes 4718596 | tf_op jit(solution)/shard_map/while
  601.3 72.3 %reduce-scatter.7.cloned.1.call-start = ((), (), s32[]{:S(2)}) async-start(), calls=%async_computation.9 | async-start | bytes 1769472 | tf_op jit(solution)/shard_map/reduce_scatter | solution.py:230
  606.4 130.2 %reduce-scatter.11.cloned.1.call-start = ((), (), s32[]{:S(2)}) async-start(), calls=%async_computation.13 | async-start | bytes 7077888 | tf_op jit(solution)/shard_map/reduce_scatter | solution.py:236
  617.3 232.8 %reduce-scatter.9.cloned.1.call-start = ((), (), s32[]{:S(2)}) async-start(), calls=%async_computation.11 | async-start | bytes 14155776 | tf_op jit(solution)/shard_map/reduce_scatter | solution.py:233
  635.1 406.1 %all-reduce.3.cloned.1.call-start = ((), (), s32[]{:S(2)}) async-start(), calls=%async_computation.16 | async-start | bytes 18874368 | tf_op jit(solution)/shard_map/psum | solution.py:241
  850.2 302.9 %all-gather.19.cloned.1.call-start = ((), (), s32[]{:S(2)}) async-start(), calls=%async_computation.10 | async-start | bytes 1769472 | tf_op jit(solution)/shard_map/all_gather | solution.py:270
  860.2 181.0 %copy-start.16 = (f32[384,768]{1,0:T(8,128)S(1)}, f32[384,768]{1,0:T(8,128)}, u32[]{:S(2)}) copy-start(f32[384,768]{1,0:T(8,128)} %param.26) | copy-start | bytes 3538948
  860.2 181.0 %copy-start.26 = (f32[384,768]{1,0:T(8,128)S(1)}, f32[384,768]{1,0:T(8,128)}, u32[]{:S(2)}) copy-start(f32[384,768]{1,0:T(8,128)} %param.27) | copy-start | bytes 3538948
  860.2 181.0 %copy-start.27 = (f32[384,768]{1,0:T(8,128)S(1)}, f32[384,768]{1,0:T(8,128)}, u32[]{:S(2)}) copy-start(f32[384,768]{1,0:T(8,128)} %param.28) | copy-start | bytes 3538948
  1044.6 108.5 %all-gather.17.cloned.1.call-start = ((), (), s32[]{:S(2)}) async-start(), calls=%async_computation.8 | async-start | bytes 5308416 | tf_op jit(solution)/shard_map/all_gather | solution.py:269
  1052.3 131.7 %all-gather.23.cloned.1.call-start = ((), (), s32[]{:S(2)}) async-start(), calls=%async_computation.14 | async-start | bytes 7077888 | tf_op jit(solution)/shard_map/all_gather | solution.py:272
  1063.3 240.8 %all-gather.21.cloned.1.call-start = ((), (), s32[]{:S(2)}) async-start(), calls=%async_computation.12 | async-start | bytes 14155776 | tf_op jit(solution)/shard_map/all_gather | solution.py:271
  1153.0 151.1 %copy-start.28 = (bf16[768,768]{1,0:T(8,128)(2,1)S(1)}, bf16[768,768]{1,0:T(8,128)(2,1)}, u32[]{:S(2)}) copy-start(bf16[768,768]{1,0:T(8,128)(2,1)} %all-gather.19.cloned.1.call-done) | copy-start | bytes 3538948
  (38 other events, 147.9 us)
Sparse Core Ops, SparseCore 0:
  10.9 52.0 all-gather.8
  65.1 22.7 all-gather.10
  90.0 117.9 all-gather.12
  210.0 62.6 all-gather.14
  601.4 47.6 reduce-scatter.12
  651.9 21.7 reduce-scatter.6
  676.5 59.9 reduce-scatter.10
  739.5 110.5 reduce-scatter.8
  855.3 185.9 all-reduce.2
  1044.7 22.8 all-gather.18
  1069.1 49.9 all-gather.16
  1120.5 63.3 all-gather.22
  1186.0 117.9 all-gather.20
where the time goes:
time: 1340 us; the launch traced here: 1330 us
  waiting for transfers between devices  626 us (47%)
  matrix products  291 us (22%)
  local copies, waits for them, and re-layouts  181 us (14%)
  other arithmetic  171 us (13%)
  blocking collectives  40.6 us (3%)
  between operations  15 us (1%)
    psum x1, waiting for transfers between devices, shards(): lax.psum(qkv_part.astype(jnp.bfloat16), 'dp').astype(jnp.float32)  175 us
    all_gather x1, waiting for transfers between devices, shards(): lax.all_gather(upd_gate_up.astype(jnp.bfloat16), 'shard', axis=0, tiled=T...  120 us
    reduce_scatter x1, waiting for transfers between devices, shards(): lax.psum_scatter(gate_up_grad.astype(jnp.bfloat16), 'shard', scatter_dime...  114 us
    unnamed x115, local copies, waits for them, and re-layouts  78.5 us
    dynamic_update_slice x4, local copies, waits for them, and re-layouts, attend_backward(): lax.scan(one_block, (zeros_acc, zeros_acc), shaped)  63.5 us
    reduce_scatter x1, waiting for transfers between devices, shards(): lax.psum_scatter(down_grad.astype(jnp.bfloat16), 'shard', scatter_dimensi...  62.9 us
    dot_general x4, matrix products, back_dot(): lax.dot_general(grad_rows, weight, (((1,), (1,)), ((), ())), preferred_el...  53.8 us
    dot_general x4, matrix products, one_block(): jnp.einsum('qhd,khd->hqk', query_block, key_rows, preferred_element_type=...  43.5 us
  transfers between devices with their start and end apart: 13, of which 10 were waited for; matrix products, arithmetic and copies ran while one was open for 22% of the time, Pallas kernels for 0%

commit v1 on v0

v1 whole, which is shorter than its diff:
```python
import functools
import math

import jax
import jax.numpy as jnp
import numpy as np
from jax import lax
from jax.experimental import pallas as pl
from jax.experimental.pallas import tpu as pltpu
from jax.sharding import PartitionSpec as P

HEADS = 12
HEAD_DIM = 64
STEP = 3

norm_eps = 1e-12
rope_base = 1000.0
learn_rate = 0.03
norm_rate = 0.3
decay_rate = 0.1
adam_eps = 1e-08
beta_first = 0.5
beta_second = 0.5

f32, bf16 = jnp.float32, jnp.bfloat16
VMEM_BYTES = 56 * 2**20


def contract(left, right, left_dim, right_dim):
    return lax.dot_general(
        left, right, (((left_dim,), (right_dim,)), ((), ())), preferred_element_type=f32
    )


def params(**more):
    return pltpu.CompilerParams(vmem_limit_bytes=VMEM_BYTES, **more)


def cost(flops, moved, transcendentals=0):
    return pl.CostEstimate(
        flops=int(flops), bytes_accessed=int(moved), transcendentals=int(transcendentals)
    )


def whole(*shape):
    return pl.BlockSpec(shape, lambda *_: (0,) * len(shape))


def rope_tables(length):
    half = HEAD_DIM // 2
    frequency = np.float32(rope_base) ** (
        -(np.arange(half, dtype=np.float32) * np.float32(2.0 / HEAD_DIM))
    )
    angles = np.arange(length, dtype=np.float32)[None, :] * frequency[:, None]
    return jnp.asarray(np.cos(angles), f32), jnp.asarray(np.sin(angles), f32)


def qkv_kernel(blocks_rotated, heads_block, tokens, weight, cosine, sine, joined):
    step = pl.program_id(0)
    rows = contract(weight[...], tokens[...], 0, 1)
    half = HEAD_DIM // 2

    @pl.when(step < 2 * blocks_rotated)
    def _():
        scale = jnp.where(step < blocks_rotated, 1.0 / math.sqrt(HEAD_DIM), 1.0)
        cos, sin = cosine[...] * scale, sine[...] * scale
        for head in range(heads_block):
            low = head * HEAD_DIM
            t1, t2 = rows[low : low + half], rows[low + half : low + 2 * half]
            joined[low : low + half] = (t1 * cos - t2 * sin).astype(bf16)
            joined[low + half : low + 2 * half] = (t2 * cos + t1 * sin).astype(bf16)

    @pl.when(step >= 2 * blocks_rotated)
    def _():
        joined[...] = rows.astype(bf16)


def project_qkv(tokens, weight, cosine, sine):
    length, width = tokens.shape
    heads_block = 4
    block = heads_block * HEAD_DIM
    count = weight.shape[1] // block
    return pl.pallas_call(
        functools.partial(qkv_kernel, count // 3, heads_block),
        grid=(count,),
        in_specs=[
            whole(length, width),
            pl.BlockSpec((width, block), lambda i: (0, i)),
            whole(*cosine.shape),
            whole(*sine.shape),
        ],
        out_specs=pl.BlockSpec((block, length), lambda i: (i, 0)),
        out_shape=jax.ShapeDtypeStruct((weight.shape[1], length), bf16),
        compiler_params=params(),
        cost_estimate=cost(2 * length * width * weight.shape[1], 2 * weight.size * 3),
        name="qkv_rope",
    )(tokens, weight, cosine, sine)


def attend_kernel(chunk, queries, key_rows, value_rows, mixed, weights):
    length = queries.shape[1]
    for low in range(0, length, chunk):
        span = pl.ds(low, chunk)
        scores = contract(key_rows[...], queries[:, span], 0, 0)
        highest = jnp.max(scores, axis=0, keepdims=True)
        expanded = jnp.exp(scores - highest)
        totals = jnp.sum(expanded, axis=0, keepdims=True)
        soft = (expanded * (1.0 / totals)).astype(bf16)
        weights[0, :, span] = soft
        mixed[:, span] = contract(value_rows[...], soft, 1, 0).astype(bf16)


def attend_forward(joined):
    length = joined.shape[1]
    head_rows = lambda part: pl.BlockSpec(
        (HEAD_DIM, length), lambda h: (part * HEADS + h, 0)
    )
    return pl.pallas_call(
        functools.partial(attend_kernel, min(256, length)),
        grid=(HEADS,),
        in_specs=[head_rows(0), head_rows(1), head_rows(2)],
        out_specs=[
            pl.BlockSpec((HEAD_DIM, length), lambda h: (h, 0)),
            pl.BlockSpec((1, length, length), lambda h: (h, 0, 0)),
        ],
        out_shape=[
            jax.ShapeDtypeStruct((HEADS * HEAD_DIM, length), bf16),
            jax.ShapeDtypeStruct((HEADS, length, length), bf16),
        ],
        compiler_params=params(),
        cost_estimate=cost(
            16 * HEADS * length * length * HEAD_DIM, 2 * HEADS * length * length, length * length * HEADS
        ),
        name="attend_forward",
    )(joined, joined, joined)


def attend_back_kernel(
    chunk,
    queries,
    key_rows,
    value_rows,
    mixed,
    grad_mixed,
    weights,
    cosine,
    sine,
    query_out,
    key_out,
    value_out,
):
    length = queries.shape[1]
    half = HEAD_DIM // 2
    grad = grad_mixed[...]
    centre = jnp.sum(grad.astype(f32) * mixed[...].astype(f32), axis=0, keepdims=True)
    query_grad = jnp.zeros((HEAD_DIM, length), f32)
    key_parts = []
    for low in range(0, length, chunk):
        span = pl.ds(low, chunk)
        soft = weights[0, span, :]
        weight_grad = contract(value_rows[:, span], grad, 0, 0)
        score_grad = (soft.astype(f32) * (weight_grad - centre)).astype(bf16)
        value_out[:, span] = contract(grad, soft, 1, 1).astype(bf16)
        key_parts.append(contract(queries[...], score_grad, 1, 1))
        query_grad += contract(key_rows[:, span], score_grad, 1, 0)
    key_grad = jnp.concatenate(key_parts, axis=1)
    cos, sin = cosine[...], sine[...]
    scale = 1.0 / math.sqrt(HEAD_DIM)
    for out, grad_rows, factor in ((query_out, query_grad, scale), (key_out, key_grad, 1.0)):
        d1, d2 = grad_rows[:half], grad_rows[half:]
        out[:half] = ((d1 * cos + d2 * sin) * factor).astype(bf16)
        out[half:] = ((d2 * cos - d1 * sin) * factor).astype(bf16)


def attend_backward(joined, mixed, grad_mixed, weights, cosine, sine):
    length = joined.shape[1]
    head_rows = lambda part: pl.BlockSpec(
        (HEAD_DIM, length), lambda h: (part * HEADS + h, 0)
    )
    rows = jax.ShapeDtypeStruct((HEADS * HEAD_DIM, length), bf16)
    return pl.pallas_call(
        functools.partial(attend_back_kernel, min(256, length)),
        grid=(HEADS,),
        in_specs=[
            head_rows(0),
            head_rows(1),
            head_rows(2),
            head_rows(0),
            head_rows(0),
            pl.BlockSpec((1, length, length), lambda h: (h, 0, 0)),
            whole(*cosine.shape),
            whole(*sine.shape),
        ],
        out_specs=[head_rows(0)] * 3,
        out_shape=[rows] * 3,
        compiler_params=params(),
        cost_estimate=cost(
            32 * HEADS * length * length * HEAD_DIM, 2 * HEADS * length * length
        ),
        name="attend_backward",
    )(joined, joined, joined, mixed, grad_mixed, weights, cosine, sine)


def norm_rows(values):
    centred = values - jnp.mean(values, axis=1, keepdims=True)
    inverse = lax.rsqrt(jnp.mean(centred * centred, axis=1, keepdims=True) + norm_eps)
    return centred * inverse, inverse


def norm_back(grad_rows, normed, inverse, gain_row):
    scaled = grad_rows * gain_row
    centred = (
        scaled
        - jnp.mean(scaled, axis=1, keepdims=True)
        - normed * jnp.mean(scaled * normed, axis=1, keepdims=True)
    )
    gain = jnp.sum(grad_rows * normed, axis=0, keepdims=True)
    bias = jnp.sum(grad_rows, axis=0, keepdims=True)
    return centred * inverse, gain, bias


def out_kernel(tokens, mixed, weight, norms, normed, inverse, hidden_low):
    sums = tokens[...].astype(f32) + contract(mixed[...], weight[...], 0, 0)
    rows, scale = norm_rows(sums)
    normed[...] = rows
    inverse[...] = scale
    hidden_low[...] = (rows * norms[0:1, :] + norms[1:2, :]).astype(bf16)


def project_out(tokens, mixed, weight, norms):
    length, width = tokens.shape
    block = min(256, length)
    return pl.pallas_call(
        out_kernel,
        grid=(length // block,),
        in_specs=[
            pl.BlockSpec((block, width), lambda i: (i, 0)),
            pl.BlockSpec((width, block), lambda i: (0, i)),
            whole(width, width),
            whole(*norms.shape),
        ],
        out_specs=[
            pl.BlockSpec((block, width), lambda i: (i, 0)),
            pl.BlockSpec((block, 1), lambda i: (i, 0)),
            pl.BlockSpec((block, width), lambda i: (i, 0)),
        ],
        out_shape=[
            jax.ShapeDtypeStruct((length, width), f32),
            jax.ShapeDtypeStruct((length, 1), f32),
            jax.ShapeDtypeStruct((length, width), bf16),
        ],
        compiler_params=params(),
        cost_estimate=cost(2 * length * width * width, 10 * length * width),
        name="out_norm",
    )(tokens, mixed, weight, norms)


def forward_kernel(
    rows_block,
    hidden_low,
    gate_weight,
    up_weight,
    down_weight,
    normed_one,
    norms,
    cotangent,
    gate,
    up,
    output,
    grad_second,
    grad_low,
    norm_grads,
    total,
):
    step = pl.program_id(0)
    length = hidden_low.shape[0]
    for low in range(0, length, rows_block):
        span = pl.ds(low, rows_block)
        gate_part = contract(hidden_low[span, :], gate_weight[...], 1, 0)
        up_part = contract(hidden_low[span, :], up_weight[...], 1, 0)
        gate[span, :] = gate_part
        up[span, :] = up_part
        inner = (gate_part * jax.nn.sigmoid(gate_part) * up_part).astype(bf16)
        part = contract(inner, down_weight[...], 1, 0)

        @pl.when(step == 0)
        def _():
            total[span, :] = part

        @pl.when(step > 0)
        def _():
            total[span, :] += part

    @pl.when(step == pl.num_programs(0) - 1)
    def _():
        gain_sum = jnp.zeros((1, total.shape[1]), f32)
        bias_sum = jnp.zeros((1, total.shape[1]), f32)
        for low in range(0, length, rows_block):
            span = pl.ds(low, rows_block)
            hidden = normed_one[span, :] * norms[0:1, :] + norms[1:2, :]
            rows, inverse = norm_rows(hidden + total[span, :])
            output[span, :] = (rows * norms[2:3, :] + norms[3:4, :]).astype(bf16)
            back, gain, bias = norm_back(
                cotangent[span, :].astype(f32), rows, inverse, norms[2:3, :]
            )
            grad_second[span, :] = back
            grad_low[span, :] = back.astype(bf16)
            gain_sum += gain
            bias_sum += bias
        norm_grads[0:1, :] = gain_sum
        norm_grads[1:2, :] = bias_sum


def feed_forward(hidden_low, gate_up, down, normed_one, norms, cotangent):
    length, width = hidden_low.shape
    inner = down.shape[0]
    block = min(512, inner)
    count = inner // block
    return pl.pallas_call(
        functools.partial(forward_kernel, min(256, length)),
        grid=(count,),
        in_specs=[
            whole(length, width),
            pl.BlockSpec((width, block), lambda j: (0, j)),
            pl.BlockSpec((width, block), lambda j: (0, count + j)),
            pl.BlockSpec((block, width), lambda j: (j, 0)),
            whole(length, width),
            whole(*norms.shape),
            whole(length, width),
        ],
        out_specs=[
            pl.BlockSpec((length, block), lambda j: (0, j)),
            pl.BlockSpec((length, block), lambda j: (0, j)),
            whole(length, width),
            whole(length, width),
            whole(length, width),
            whole(2, width),
        ],
        out_shape=[
            jax.ShapeDtypeStruct((length, inner), f32),
            jax.ShapeDtypeStruct((length, inner), f32),
            jax.ShapeDtypeStruct((length, width), bf16),
            jax.ShapeDtypeStruct((length, width), f32),
            jax.ShapeDtypeStruct((length, width), bf16),
            jax.ShapeDtypeStruct((2, width), f32),
        ],
        scratch_shapes=[pltpu.VMEM((length, width), f32)],
        compiler_params=params(),
        cost_estimate=cost(6 * length * width * inner, 8 * length * inner),
        name="feed_forward",
    )(hidden_low, gate_up, gate_up, down, normed_one, norms, cotangent)


def backward_kernel(
    rows_block,
    last,
    grad_low,
    hidden_low,
    gate,
    up,
    gate_weight,
    up_weight,
    down_weight,
    before,
    normed,
    inverse,
    norms,
    gate_out,
    up_out,
    down_out,
    *rest,
):
    step = pl.program_id(0)
    length = hidden_low.shape[0]
    if last:
        grad_first, first_low, norm_grads, total, inner, gate_back, up_back = rest
    else:
        grad_hidden, total, inner, gate_back, up_back = rest

    @pl.when(step == 0)
    def _():
        total[...] = before[...]

    for low in range(0, length, rows_block):
        span = pl.ds(low, rows_block)
        inner_grad = contract(grad_low[span, :], down_weight[...], 1, 1)
        gate_part, up_part = gate[span, :], up[span, :]
        sigmoid = jax.nn.sigmoid(gate_part)
        swished = gate_part * sigmoid
        inner[span, :] = (swished * up_part).astype(bf16)
        gate_grad = inner_grad * up_part * sigmoid * (1.0 + gate_part * (1.0 - sigmoid))
        gate_low, up_low = gate_grad.astype(bf16), (inner_grad * swished).astype(bf16)
        gate_back[span, :] = gate_low
        up_back[span, :] = up_low
        total[span, :] += contract(gate_low, gate_weight[...], 1, 1) + contract(
            up_low, up_weight[...], 1, 1
        )
    down_out[...] = contract(inner[...], grad_low[...], 0, 0).astype(bf16)
    gate_out[...] = contract(hidden_low[...], gate_back[...], 0, 0).astype(bf16)
    up_out[...] = contract(hidden_low[...], up_back[...], 0, 0).astype(bf16)

    @pl.when(step == pl.num_programs(0) - 1)
    def _():
        if not last:
            grad_hidden[...] = total[...]
            return
        gain_sum = jnp.zeros((1, total.shape[1]), f32)
        bias_sum = jnp.zeros((1, total.shape[1]), f32)
        for low in range(0, length, rows_block):
            span = pl.ds(low, rows_block)
            back, gain, bias = norm_back(
                total[span, :], normed[span, :], inverse[span, :], norms[0:1, :]
            )
            grad_first[span, :] = back
            first_low[span, :] = back.astype(bf16)
            gain_sum += gain
            bias_sum += bias
        norm_grads[0:1, :] = gain_sum
        norm_grads[1:2, :] = bias_sum


def feed_backward(
    piece,
    pieces,
    groups,
    grad_low,
    hidden_low,
    gate,
    up,
    gate_up,
    down,
    before,
    normed,
    inverse,
    norms,
):
    length, width = hidden_low.shape
    inner = down.shape[0]
    block = 256
    count = inner // block
    run = count // (groups * pieces)
    last = piece == pieces - 1

    def place(j):
        return (j // run) * (count // groups) + piece * run + j % run

    in_cols = lambda shift: pl.BlockSpec((width, block), lambda j: (0, shift + place(j)))
    wide = pl.BlockSpec((length, block), lambda j: (0, place(j)))
    part = inner // pieces
    outs = [
        (pl.BlockSpec((width, block), lambda j: (0, j)), jax.ShapeDtypeStruct((width, part), bf16)),
        (pl.BlockSpec((width, block), lambda j: (0, j)), jax.ShapeDtypeStruct((width, part), bf16)),
        (pl.BlockSpec((block, width), lambda j: (j, 0)), jax.ShapeDtypeStruct((part, width), bf16)),
    ]
    full = whole(length, width)
    if last:
        outs += [
            (full, jax.ShapeDtypeStruct((length, width), f32)),
            (full, jax.ShapeDtypeStruct((length, width), bf16)),
            (whole(2, width), jax.ShapeDtypeStruct((2, width), f32)),
        ]
    else:
        outs += [(full, jax.ShapeDtypeStruct((length, width), f32))]
    return pl.pallas_call(
        functools.partial(backward_kernel, min(256, length), last),
        grid=(groups * run,),
        in_specs=[
            full,
            full,
            wide,
            wide,
            in_cols(0),
            in_cols(count),
            pl.BlockSpec((block, width), lambda j: (place(j), 0)),
            full,
            full,
            whole(length, 1),
            whole(*norms.shape),
        ],
        out_specs=[spec for spec, _ in outs],
        out_shape=[shape for _, shape in outs],
        scratch_shapes=[pltpu.VMEM((length, width), f32)] + [pltpu.VMEM((length, block), bf16)] * 3,
        compiler_params=params(),
        cost_estimate=cost(12 * length * width * part, 8 * length * part),
        name="feed_backward",
    )(grad_low, hidden_low, gate, up, gate_up, gate_up, down, before, normed, inverse, norms)


class Links:
    def __init__(self, mesh):
        self.sizes = {"dp": mesh.shape["dp"], "shard": mesh.shape["shard"]}
        chips = self.sizes["dp"] // 2
        near = 2 if chips % 2 == 0 else 1
        self.core = ("dp", 1, 2)
        self.near = ("dp", 2, near)
        self.far = ("dp", 2 * near, chips // near)
        self.shard = ("shard", 1, self.sizes["shard"])

    def place(self, digit):
        axis, stride, size = digit
        return (lax.axis_index(axis) // stride) % size

    def shift(self, value, digit, step):
        axis, stride, size = digit
        pairs = []
        for i in range(self.sizes[axis]):
            own = (i // stride) % size
            pairs.append((i, i + ((own + step) % size - own) * stride))
        return lax.ppermute(value, axis, pairs)

    def scatter_sum(self, value, digit, dim):
        size = digit[2]
        if size == 1:
            return value
        own = self.place(digit)
        width = value.shape[dim] // size

        def piece(index):
            return lax.dynamic_slice_in_dim(value, index * width, width, dim)

        total = piece(own).astype(f32)
        for step in range(1, size):
            total += self.shift(piece((own + step) % size), digit, step).astype(f32)
        return total.astype(bf16)

    def gather(self, value, digit, dim):
        size = digit[2]
        if size == 1:
            return value
        own = self.place(digit)
        width = value.shape[dim]
        if size == 2:
            other = self.shift(value, digit, 1)
            first = jnp.where(own == 0, value, other)
            second = jnp.where(own == 0, other, value)
            return jnp.concatenate([first, second], axis=dim)
        shape = list(value.shape)
        shape[dim] *= size
        full = lax.dynamic_update_slice_in_dim(
            jnp.zeros(shape, value.dtype), value, own * width, dim
        )
        for step in range(1, size):
            came = self.shift(value, digit, step)
            full = lax.dynamic_update_slice_in_dim(
                full, came, ((own - step) % size) * width, dim
            )
        return full

    def gather_rows(self, value, spread):
        parts = [self.core, self.near] if spread else [self.core]
        piece = value
        for digit in parts:
            width = piece.shape[0] // digit[2]
            piece = lax.dynamic_slice_in_dim(piece, self.place(digit) * width, width, 0)
        size = self.shard[2]
        rows = value.shape[0]
        own = self.place(self.shard)
        full = lax.dynamic_update_slice_in_dim(
            jnp.zeros((size * rows, value.shape[1]), value.dtype), value, own * rows, 0
        )
        for step in range(1, size):
            came = self.shift(piece, self.shard, step)
            for digit in reversed(parts):
                came = self.gather(came, digit, 0)
            full = lax.dynamic_update_slice_in_dim(full, came, ((own - step) % size) * rows, 0)
        return full

    def total(self, grads):
        grads = self.scatter_sum(grads, self.core, 1)
        grads = self.scatter_sum(grads, self.shard, 0)
        grads = self.scatter_sum(grads, self.near, 0)
        grads = self.scatter_sum(grads, self.far, 0)
        grads = self.gather(grads, self.far, 0)
        grads = self.gather(grads, self.near, 0)
        return self.gather(grads, self.core, 1)


def adam_update(weight, first_moment, second_moment, gradient, rate, decay_on):
    first_new = beta_first * first_moment + (1.0 - beta_first) * gradient
    second_new = beta_second * second_moment + (1.0 - beta_second) * gradient * gradient
    fix_first = 1.0 - beta_first**STEP
    fix_second = 1.0 - beta_second**STEP
    direction = first_new / fix_first / (jnp.sqrt(second_new / fix_second) + adam_eps)
    return (weight - rate * (direction + decay_on * weight), first_new, second_new)


class Finish:
    def __init__(self, mesh, shapes, plan, scale):
        self.far_size = mesh.shape["dp"] // 4
        self.scale = scale
        self.shapes = shapes
        self.plan = plan

    @staticmethod
    def fits(mesh, rows):
        far = mesh.shape["dp"] // 4
        return (
            mesh.shape["shard"] == 2
            and mesh.shape["dp"] % 4 == 0
            and all(count % (2 * far * 16) == 0 for count in rows)
        )

    def chunk_scratch(self):
        first, own, second, third, fourth, totals = [], [], [], [], [], []
        for _, _, _, width, _, _, rows in self.plan:
            near, far = rows // 2, rows // 2 // self.far_size
            first.append(pltpu.VMEM((2 * rows, width), bf16))
            own.append(pltpu.VMEM((2 * rows, width), bf16))
            second.append(pltpu.VMEM((rows, width), bf16))
            third.append(pltpu.VMEM((near, width), bf16))
            fourth.append(pltpu.VMEM((max(self.far_size - 1, 1), far, width), bf16))
            totals.append(pltpu.VMEM((2, rows, width), bf16))
        return first + own + second + third + fourth + totals

    def __call__(self, grads, masters, norm_grads, norm_state):
        count, matrices = len(self.plan), len(masters)
        self.block_rows = min(rows for *_, rows in self.plan)
        self.block_cols = max(width for _, _, _, width, *_ in self.plan)
        self.blocks = [
            (k, half, low)
            for k, chunk in enumerate(self.plan)
            for half in range(2)
            for low in range(0, chunk[6], self.block_rows)
        ]
        block = (2, self.block_rows, self.block_cols)
        far = max(self.far_size - 1, 1)
        dma = pltpu.SemaphoreType.DMA
        scratch = self.chunk_scratch() + [
            pltpu.VMEM((3,) + block, f32),
            pltpu.VMEM((2,) + block, f32),
            pltpu.VMEM(block, bf16),
            pltpu.VMEM((3,) + norm_grads.shape, f32),
            pltpu.VMEM((self.far_size,) + norm_grads.shape, f32),
            dma((count,)),
            dma((9, count, 2)),
            dma((2, count, far, 2)),
            dma((4 + 2 * far,)),
            dma((3 + far,)),
            dma((2, 3)),
            dma((2, 4)),
        ]
        anywhere = pl.BlockSpec(memory_space=pl.ANY)
        in_vmem = pl.BlockSpec(memory_space=pltpu.VMEM)
        state = [part for master in masters for part in master]
        outs = []
        for master, _, _ in masters:
            full = (2 * master.shape[0], master.shape[1])
            outs += [
                jax.ShapeDtypeStruct(full, bf16),
                jax.ShapeDtypeStruct(master.shape, f32),
                jax.ShapeDtypeStruct(master.shape, f32),
            ]
        norm_outs = [jax.ShapeDtypeStruct(norm_grads.shape, f32)] * 3
        results = pl.pallas_call(
            functools.partial(self.kernel, len(grads), matrices),
            in_specs=[anywhere] * (len(grads) + len(state)) + [in_vmem] * 4,
            out_specs=[anywhere] * len(outs) + [in_vmem] * 3,
            out_shape=outs + norm_outs,
            scratch_shapes=scratch,
            compiler_params=params(collective_id=1, has_side_effects=True),
            name="finish",
        )(*grads, *state, norm_grads, *norm_state)
        updated = [tuple(results[3 * i : 3 * i + 3]) for i in range(matrices)]
        return updated, tuple(results[3 * matrices :])

    def kernel(self, grad_count, matrices, *refs):
        refs = list(refs)

        def take(number):
            taken = refs[:number]
            del refs[:number]
            return taken

        count = len(self.plan)
        grads, state = take(grad_count), take(3 * matrices)
        norm_in, norms, norm_first, norm_second = take(4)
        outs, norm_outs = take(3 * matrices), take(3)
        first, own, second, third, fourth, totals = [take(count) for _ in range(6)]
        load_buf, store_buf, new_buf, norm_sum, norm_far = take(5)
        own_sem, pair_sem, far_sem, norm_send, norm_recv, load_sem, store_sem = take(7)

        dp, shard = lax.axis_index("dp"), lax.axis_index("shard")
        core, near, far = dp % 2, dp // 2 % 2, dp // 4
        sizes = self.far_size
        core_peer, near_peer, shard_peer = (dp + 1 - 2 * core, shard), (dp + 2 - 4 * near, shard), (dp, 1 - shard)

        def far_peer(step):
            return (dp + ((far + step) % sizes - far) * 4, shard)

        peers = [core_peer, near_peer, shard_peer] + [far_peer(step) for step in range(1, sizes)]
        barrier = pltpu.get_barrier_semaphore()
        for peer in peers:
            pl.semaphore_signal(barrier, inc=1, device_id=peer, device_id_type=pl.DeviceIdType.MESH)
        pl.semaphore_wait(barrier, len(peers))

        pending = []

        def send(source, target, sent, came, peer):
            copy = pltpu.make_async_remote_copy(
                src_ref=source,
                dst_ref=target,
                send_sem=sent,
                recv_sem=came,
                device_id=peer,
                device_id_type=pl.DeviceIdType.MESH,
            )
            copy.start()
            pending.append(copy)
            return copy

        def pair(stage, k, source, target, peer):
            return send(source, target, pair_sem.at[stage, k, 0], pair_sem.at[stage, k, 1], peer)

        def columns(k, half, total):
            _, before, low, width, *_ = self.plan[k]
            return pl.ds(pl.multiple_of(half * (total // 2) + low, 128), width)

        def add_rows(target, sources, rows, step):
            @pl.loop(0, rows // step)
            def _(i):
                span = pl.ds(pl.multiple_of(i * step, step), step)
                value = sources[0][span, :].astype(f32)
                for source in sources[1:]:
                    value += source[span, :].astype(f32)
                target[span, :] = value.astype(bf16)

        copies = {}

        def start_core(k):
            grad, total, _, width, _, _, rows = self.plan[k]
            load = pltpu.make_async_copy(grads[grad].at[:, columns(k, core, total)], own[k], own_sem.at[k])
            load.start()
            copies["own", k] = load
            copies["core", k] = pair(
                0, k, grads[grad].at[:, columns(k, 1 - core, total)], first[k], core_peer
            )

        def start_shard(k):
            rows = self.plan[k][6]
            copies["own", k].wait()
            copies["core", k].wait_recv()
            add_rows(own[k], [own[k], first[k]], 2 * rows, 16)
            copies["shard", k] = pair(
                1, k, own[k].at[pl.ds(pl.multiple_of((1 - shard) * rows, 16), rows)], second[k], shard_peer
            )

        def start_near(k):
            rows = self.plan[k][6]
            half = rows // 2
            copies["shard", k].wait_recv()
            add_rows(
                second[k], [second[k], own[k].at[pl.ds(pl.multiple_of(shard * rows, 16), rows)]], rows, 16
            )
            copies["near", k] = pair(
                2, k, second[k].at[pl.ds(pl.multiple_of((1 - near) * half, 16), half)], third[k], near_peer
            )

        def start_far(k):
            half = self.plan[k][6] // 2
            part = half // sizes
            copies["near", k].wait_recv()
            add_rows(
                third[k], [third[k], second[k].at[pl.ds(pl.multiple_of(near * half, 16), half)]], half, 16
            )
            for step in range(1, sizes):
                place = pl.multiple_of((far + step) % sizes * part, 16)
                copies["far", k, step] = send(
                    third[k].at[pl.ds(place, part)],
                    fourth[k].at[step - 1],
                    far_sem.at[0, k, step - 1, 0],
                    far_sem.at[0, k, step - 1, 1],
                    far_peer(step),
                )

        def own_part(k):
            half = self.plan[k][6] // 2
            part = half // sizes
            return totals[k].at[core, pl.ds(pl.multiple_of(near * half + far * part, 16), part)]

        def start_far_total(k):
            part = self.plan[k][6] // 2 // sizes
            for step in range(1, sizes):
                copies["far", k, step].wait_recv()
            add_rows(
                own_part(k),
                [third[k].at[pl.ds(pl.multiple_of(far * part, 16), part)]]
                + [fourth[k].at[step - 1] for step in range(1, sizes)],
                part,
                16,
            )
            for step in range(1, sizes):
                copies["far total", k, step] = send(
                    own_part(k),
                    own_part(k),
                    far_sem.at[1, k, step - 1, 0],
                    far_sem.at[1, k, step - 1, 1],
                    far_peer(step),
                )

        def start_near_total(k):
            half = self.plan[k][6] // 2
            for step in range(1, sizes):
                copies["far total", k, step].wait_recv()
            rows = totals[k].at[core, pl.ds(pl.multiple_of(near * half, 16), half)]
            copies["near total", k] = pair(3, k, rows, rows, near_peer)

        def start_core_total(k):
            copies["near total", k].wait_recv()
            copies["core total", k] = pair(4, k, totals[k].at[core], totals[k].at[core], core_peer)

        def places(b):
            k, half, low = self.blocks[b]
            _, total, start, width, matrix, before, rows = self.plan[k]
            column = before + half * (total // 2) + start
            return k, half, low, matrix, pl.ds(low, self.block_rows), pl.ds(column, width), width, rows

        def load(b):
            _, _, _, matrix, rows, cols, width, _ = places(b)
            for i in range(3):
                copy = pltpu.make_async_copy(
                    state[3 * matrix + i].at[rows, cols],
                    load_buf.at[i, b % 2, :, pl.ds(0, width)],
                    load_sem.at[b % 2, i],
                )
                copy.start()
                copies["load", b, i] = copy

        def settle(b, first):
            while len(copies["store", b]) > 3 - first:
                copies["store", b].pop(0).wait()

        def update(b):
            k, half, low, matrix, rows, cols, width, shard_rows = places(b)
            slot = b % 2
            for i in range(3):
                copies["load", b, i].wait()
            if b >= 2:
                settle(b - 2, 3)

            step = 16

            @pl.loop(0, self.block_rows // step)
            def _(i):
                span = pl.ds(pl.multiple_of(i * step, step), step)
                lanes = pl.ds(0, width)
                grad = totals[k][half, pl.ds(pl.multiple_of(low + i * step, step), step), :]
                grad = grad.astype(f32) * self.scale
                new, first_new, second_new = adam_update(
                    load_buf[0, slot, span, lanes],
                    load_buf[1, slot, span, lanes],
                    load_buf[2, slot, span, lanes],
                    grad,
                    learn_rate,
                    decay_rate,
                )
                store_buf[0, slot, span, lanes] = first_new
                store_buf[1, slot, span, lanes] = second_new
                new_buf[slot, span, lanes] = new.astype(bf16)

            lanes = pl.ds(0, width)
            stores = []
            for i in range(2):
                stores.append(
                    pltpu.make_async_copy(
                        store_buf.at[i, slot, :, lanes],
                        outs[3 * matrix + 1 + i].at[rows, cols],
                        store_sem.at[slot, i],
                    )
                )
            full_rows = pl.ds(pl.multiple_of(shard * shard_rows + low, 16), self.block_rows)
            stores.append(
                pltpu.make_async_copy(
                    new_buf.at[slot, :, lanes],
                    outs[3 * matrix].at[full_rows, cols],
                    store_sem.at[slot, 2],
                )
            )
            for copy in stores:
                copy.start()
            copies["store", b] = stores[::-1]

        def region(k, half, side, low, rows):
            _, total, start, width, matrix, before, shard_rows = self.plan[k]
            column = before + half * (total // 2) + start
            return outs[3 * matrix].at[
                pl.ds(pl.multiple_of(side * shard_rows + low, 16), rows),
                pl.ds(pl.multiple_of(column, 128), width),
            ]

        def start_new(k):
            half = self.plan[k][6] // 2
            for b, (chunk, _, _) in enumerate(self.blocks):
                if chunk == k:
                    settle(b, 1)
            rows = region(k, core, shard, near * half, half)
            copies["new", k] = pair(5, k, rows, rows, shard_peer)

        def start_new_near(k):
            half = self.plan[k][6] // 2
            copies["new", k].wait_recv()
            rows = region(k, core, 1 - shard, near * half, half)
            copies["new near", k] = pair(6, k, rows, rows, near_peer)

        def start_new_core(k):
            copies["new near", k].wait_recv()
            rows = region(k, core, 1 - shard, 0, self.plan[k][6])
            copies["new core", k] = pair(7, k, rows, rows, core_peer)

        norm_copies = {}

        def norm_send_to(slot, source, peer):
            norm_copies[slot] = send(source, norm_sum.at[slot], norm_send.at[slot], norm_recv.at[slot], peer)

        def norm_stage(stage):
            if stage == 0:
                norm_send_to(0, norm_in, core_peer)
            elif stage == 1:
                norm_copies[0].wait_recv()
                norm_sum[0] += norm_in[...]
                norm_send_to(1, norm_sum.at[0], shard_peer)
            elif stage == 2:
                norm_copies[1].wait_recv()
                norm_sum[1] += norm_sum[0]
                norm_send_to(2, norm_sum.at[1], near_peer)
            elif stage == 3:
                norm_copies[2].wait_recv()
                norm_sum[2] += norm_sum[1]
                norm_far[far] = norm_sum[2]
                for step in range(1, sizes):
                    norm_copies["far", step] = send(
                        norm_sum.at[2],
                        norm_far.at[far],
                        norm_send.at[3 + step],
                        norm_recv.at[2 + step],
                        far_peer(step),
                    )
            elif stage == 4:
                total = None
                for step in range(1, sizes):
                    norm_copies["far", step].wait_recv()
                total = norm_far[0]
                for place in range(1, sizes):
                    total += norm_far[place]
                new, first_new, second_new = adam_update(
                    norms[...], norm_first[...], norm_second[...], total * self.scale, norm_rate, 0.0
                )
                norm_outs[0][...] = new
                norm_outs[1][...] = first_new
                norm_outs[2][...] = second_new

        ahead = 2
        for k in range(min(ahead + 1, count)):
            start_core(k)
        norm_stage(0)
        for k in range(min(ahead, count)):
            start_shard(k)
        load(0)
        load(1)
        done = 0

        def run_update(k):
            nonlocal done
            copies["core total", k].wait_recv()
            while done < len(self.blocks) and self.blocks[done][0] == k:
                update(done)
                if done + 2 < len(self.blocks):
                    load(done + 2)
                done += 1
            start_new(k)

        def on(k, action):
            if 0 <= k < count:
                action(k)

        for t in range(count + 6):
            on(t, start_near)
            if t < count and t + ahead < count:
                if t + ahead + 1 < count:
                    start_core(t + ahead + 1)
                start_shard(t + ahead)
            if 1 + t < 5:
                norm_stage(1 + t)
            on(t - 1, start_far)
            on(t - 2, start_core_total)
            on(t - 4, start_new_near)
            on(t - 1, start_far_total)
            on(t - 2, run_update)
            on(t - 1, start_near_total)
            on(t - 5, start_new_core)
            on(t - 6, lambda k: copies["new core", k].wait_recv())
        for copy in pending:
            copy.wait_send()
        for b in range(len(self.blocks)):
            settle(b, 3)


def shards(
    mesh,
    tokens,
    cotangent,
    master_qkv,
    first_qkv,
    second_qkv,
    master_out,
    first_out,
    second_out,
    master_gate_up,
    first_gate_up,
    second_gate_up,
    master_down,
    first_down,
    second_down,
    norms,
    norm_first,
    norm_second,
):
    links = Links(mesh)
    length, width = tokens.shape
    shard_count = mesh.shape["shard"]
    cosine, sine = rope_tables(length)

    weight_qkv = links.gather_rows(master_qkv.astype(bf16), False)
    weight_out = links.gather_rows(master_out.astype(bf16), False)
    weight_gate_up = links.gather_rows(master_gate_up.astype(bf16), True)
    weight_down = links.gather_rows(master_down.astype(bf16), True)

    joined = project_qkv(tokens, weight_qkv, cosine, sine)
    mixed, weights = attend_forward(joined)
    normed_one, inverse_one, hidden_low = project_out(tokens, mixed, weight_out, norms)
    gate, up, output, grad_second, grad_low, norm_two = feed_forward(
        hidden_low, weight_gate_up, weight_down, normed_one, norms, cotangent
    )

    inner = weight_down.shape[0]
    pieces = 1
    groups = shard_count if pieces > 1 else 1
    carried = grad_second
    for piece in range(pieces):
        gate_grad, up_grad, down_grad, carried, *more = feed_backward(
            piece,
            pieces,
            groups,
            grad_low,
            hidden_low,
            gate,
            up,
            weight_gate_up,
            weight_down,
            carried,
            normed_one,
            inverse_one,
            norms,
        )
    grad_first = carried
    first_low, norm_one = more

    out_grad = contract(mixed, first_low, 1, 0).astype(bf16)
    mixed_grad = contract(weight_out, first_low, 1, 1).astype(bf16)
    query_back, key_back, value_back = attend_backward(
        joined, mixed, mixed_grad, weights, cosine, sine
    )
    joined_back = jnp.concatenate([query_back, key_back, value_back], axis=0)
    qkv_grad = contract(tokens, joined_back, 0, 1).astype(bf16)
    input_grad = (grad_first + contract(joined_back, weight_qkv, 0, 1)).astype(bf16)

    scale_grad = 1.0 / math.sqrt(length * mesh.shape["dp"] * shard_count)
    grads = [gate_grad, up_grad, down_grad, out_grad, qkv_grad]
    masters = [
        (master_gate_up, first_gate_up, second_gate_up),
        (master_down, first_down, second_down),
        (master_out, first_out, second_out),
        (master_qkv, first_qkv, second_qkv),
    ]
    norm_grads = jnp.concatenate([norm_one, norm_two])
    norm_state = (norms, norm_first, norm_second)
    if Finish.fits(mesh, [master.shape[0] for master, _, _ in masters]):
        rows, long_rows = master_out.shape[0], master_down.shape[0]
        plan = [
            (2, width, 0, 256, 1, 0, long_rows),
            (0, inner, 0, 768, 0, 0, rows),
            (1, inner, 0, 768, 0, inner, rows),
            (0, inner, 768, 768, 0, 0, rows),
            (1, inner, 768, 768, 0, inner, rows),
            (2, width, 256, 128, 1, 0, long_rows),
            (4, 3 * width, 0, 768, 3, 0, rows),
            (4, 3 * width, 768, 384, 3, 0, rows),
            (3, width, 0, 384, 2, 0, rows),
        ]
        finish = Finish(mesh, [grad.shape for grad in grads], plan, scale_grad)
        updated, updated_norms = finish(grads, masters, norm_grads, norm_state)
    else:
        totals = [
            jnp.concatenate([links.total(gate_grad), links.total(up_grad)], axis=1),
            links.total(down_grad),
            links.total(out_grad),
            links.total(qkv_grad),
        ]
        updated = []
        for (master, first, second), total in zip(masters, totals, strict=True):
            new, first_new, second_new = adam_update(
                master, first, second, total.astype(f32) * scale_grad, learn_rate, decay_rate
            )
            updated.append((links.gather_rows(new.astype(bf16), True), first_new, second_new))
        norm_total = lax.psum(norm_grads, ("dp", "shard"))
        updated_norms = adam_update(*norm_state, norm_total * scale_grad, norm_rate, 0.0)
    (
        (full_gate_up, first_gate_up_new, second_gate_up_new),
        (full_down, first_down_new, second_down_new),
        (full_out, first_out_new, second_out_new),
        (full_qkv, first_qkv_new, second_qkv_new),
    ) = updated
    upd_norms, norm_first_new, norm_second_new = updated_norms
    return (
        output,
        input_grad,
        full_qkv,
        full_out,
        full_gate_up,
        full_down,
        first_qkv_new,
        second_qkv_new,
        first_out_new,
        second_out_new,
        first_gate_up_new,
        second_gate_up_new,
        first_down_new,
        second_down_new,
        upd_norms,
        norm_first_new,
        norm_second_new,
    )


def solution(mesh):
    rows, split, copied = P(("dp", "shard"), None), P("shard", None), P()
    return jax.shard_map(
        functools.partial(shards, mesh),
        mesh=mesh,
        in_specs=(rows, rows) + (split,) * 12 + (copied,) * 3,
        out_specs=(rows, rows) + (copied,) * 4 + (split,) * 8 + (copied,) * 3,
        check_vma=False,
    )
```

time: 1340 us -> 611 us (0.46)
  waiting for transfers between devices: 626 us -> 75.7 us
  Pallas kernels: 0 us -> 409 us
  matrix products: 291 us -> 19.2 us
  other arithmetic: 171 us -> 26.6 us
  local copies, waits for them, and re-layouts: 181 us -> 67.7 us
  blocking collectives: 40.6 us -> 0 us
  between operations: 15 us -> 1.01 us
    pallas_call x0 -> x7, Pallas kernels: none -> 409 us  [the longest x1 235 us: __call__(): pl.pallas_call(functools.partial(self.kernel, len(grads), matrices), in_s...]
    dot_general x26 -> x4, matrix products: 291 us -> 19.2 us  [contract(): lax.dot_general(left, right, (((left_dim,), (right_dim,)), ((), ())), pre...]
    all_gather x8 -> x0, waiting for transfers between devices: 240 us -> none  [the longest x1 120 us: shards(): lax.all_gather(upd_gate_up.astype(jnp.bfloat16), 'shard', axis=0, tiled=T...]
    reduce_scatter x3 -> x0, waiting for transfers between devices: 197 us -> none  [the longest x1 114 us: shards(): lax.psum_scatter(gate_up_grad.astype(jnp.bfloat16), 'shard', scatter_dime...]
    psum x1 -> x0, waiting for transfers between devices: 175 us -> none  [shards(): lax.psum(qkv_part.astype(jnp.bfloat16), 'dp').astype(jnp.float32)]
    convert_element_type x13 -> x0, other arithmetic: 122 us -> none  [the longest x2 42.8 us: one_block(): score_grad = (weights_soft * (weight_grad - centre)).astype(jnp.bfloat16)]
    ppermute x0 -> x10, waiting for transfers between devices: none -> 75.7 us  [shift(): return lax.ppermute(value, axis, pairs)]
    dynamic_update_slice x4 -> x0, local copies, waits for them, and re-layouts: 63.5 us -> none  [attend_backward(): lax.scan(one_block, (zeros_acc, zeros_acc), shaped)]
  transfers between devices with their start and end apart: 13 -> 10, of which waited for: 10 -> 3; matrix products, arithmetic and copies ran while one was open for 22% -> 4% of each run, Pallas kernels for 0% -> 10%
where the time goes in v1:
time: 611 us; the launch traced here: 609 us
  Pallas kernels  409 us (67%)
  waiting for transfers between devices  75.7 us (12%)
  local copies, waits for them, and re-layouts  67.7 us (11%)
  other arithmetic  26.6 us (4%)
  matrix products  19.2 us (3%)
  starting transfers between devices  9.62 us (2%)
    pallas_call x1, Pallas kernels, __call__(): pl.pallas_call(functools.partial(self.kernel, len(grads), matrices), in_s...  235 us
    ppermute x10, waiting for transfers between devices, shift(): return lax.ppermute(value, axis, pairs)  75.7 us
    unnamed x79, local copies, waits for them, and re-layouts  58 us
    pallas_call x1, Pallas kernels, feed_backward(): pl.pallas_call(functools.partial(backward_kernel, min(256, length), last)...  50.3 us
    pallas_call x1, Pallas kernels, attend_forward(): pl.pallas_call(functools.partial(attend_kernel, min(256, length)), grid=(...  44.4 us
    pallas_call x1, Pallas kernels, feed_forward(): pl.pallas_call(functools.partial(forward_kernel, min(256, length)), grid=...  34.8 us
    pallas_call x1, Pallas kernels, attend_backward(): pl.pallas_call(functools.partial(attend_back_kernel, min(256, length)), g...  27.4 us
    dot_general x4, matrix products, contract(): lax.dot_general(left, right, (((left_dim,), (right_dim,)), ((), ())), pre...  19.2 us
  transfers between devices with their start and end apart: 10, of which 3 were waited for; matrix products, arithmetic and copies ran while one was open for 4% of the time, Pallas kernels for 10%

profile of v1, /device:TPU:0, one launch (start us, length us, event | category | flops | bytes accessed | tf_op | source)
XLA Modules:
  0.0 609.3 jit_solution(4537005688799345064)
XLA Ops:
  0.7 2.0 broadcast_in_dim.12
  6.3 3.0 collective-permute-start
  9.6 2.0 copy-done
  12.0 2.2 copy-done.2
  15.2 4.9 broadcast_in_dim.14
  20.1 6.7 %constant_dynamic-update-slice_fusion.4 = (bf16[768,6144]{1,0:T(8,128)(2,1)}, bf16[384,6144]{1,0:T(8,128)(2,1)S(1)}) fusion(bf16[768,6144]{1,0:T(8,128)(2,1)} %broadcast_in_dim.14, s32[]{:T(128)S(6)} %select_n.181, f32[384,6144]{1,0:T(8,128)} %refs_5_.1), kind=kLoop, calls=%fused_computation.30 | loop fusion | flops 2359296 | bytes 18874372 | tf_op jit(solution)/shard_map/dynamic_update_slice | solution.py:558
  27.0 2.1 collective-permute-start.4
  30.2 43.3 %collective-permute-done.2 = bf16[192,768]{1,0:T(8,128)(2,1)} collective-permute-done((bf16[192,768]{1,0:T(8,128)(2,1)S(1)}, bf16[192,768]{1,0:T(8,128)(2,1)}, u32[]{:S(2)}, u32[]{:S(2)}) %collective-permute-start.2) | collective-permute-done | bytes 294944 | tf_op jit(solution)/shard_map/ppermute | solution.py:509
  78.4 11.6 %collective-permute-done.8 = bf16[384,768]{1,0:T(8,128)(2,1)} collective-permute-done((bf16[384,768]{1,0:T(8,128)(2,1)}, bf16[384,768]{1,0:T(8,128)(2,1)}, u32[]{:S(2)}, u32[]{:S(2)}) %collective-permute-start.8) | collective-permute-done | bytes 589856 | tf_op jit(solution)/shard_map/ppermute | solution.py:509
  93.9 20.8 %collective-permute-done.5 = bf16[96,6144]{1,0:T(8,128)(2,1)S(1)} collective-permute-done((bf16[96,6144]{1,0:T(8,128)(2,1)S(1)}, bf16[96,6144]{1,0:T(8,128)(2,1)S(1)}, u32[]{:S(2)}, u32[]{:S(2)}) %collective-permute-start.5) | collective-permute-done | bytes 1179680 | tf_op jit(solution)/shard_map/ppermute | solution.py:509
  117.9 11.0 %qkv_rope.1.queries.key_rows.value_rows = bf16[2304,1024]{1,0:T(8,128)(2,1)} custom-call(bf16[1024,768]{1,0:T(8,128)(2,1)} %tokens.3, bf16[768,2304]{1,0:T(8,128)(2,1)} %maximum_dynamic-update-slice_fusion.2.weight, f32[32,1024]{1,0:T(8,128)} %constant.159.clone.cosine, f32[32,1024]{1,0:T(8,128)} %constant.160.clone.sine), custom_call_target="tpu_custom_call" | custom-call | flops 3623878656 | bytes 10616832 | tf_op jit(solution)/shard_map/qkv_rope/pallas_call | solution.py:83
  128.8 44.4 %attend_forward.1 = (bf16[768,1024]{1,0:T(8,128)(2,1)}, bf16[12,1024,1024]{2,1,0:T(8,128)(2,1)}) custom-call(bf16[2304,1024]{1,0:T(8,128)(2,1)} %qkv_rope.1.queries.key_rows.value_rows, bf16[2304,1024]{1,0:T(8,128)(2,1)} %qkv_rope.1.queries.key_rows.value_rows, bf16[2304,1024]{1,0:T(8,128)(2,1)} %qkv_rope.1.queries.key_rows.value_rows), custom_call_target="tpu_custom_call" | custom-call | flops 12884901888 | bytes 25165824 | tf_op jit(solution)/shard_map/attend_forward/pallas_call | solution.py:118
  173.2 6.4 %out_norm.1 = (f32[1024,768]{1,0:T(8,128)}, f32[1024,1]{1,0:T(8,128)}, bf16[1024,768]{1,0:T(8,128)(2,1)}) custom-call(bf16[1024,768]{1,0:T(8,128)(2,1)} %tokens.3, bf16[768,1024]{1,0:T(8,128)(2,1)} %get-tuple-element.52.mixed, bf16[768,768]{1,0:T(8,128)(2,1)} %copy-done.12, f32[4,768]{1,0:T(4,128)} %refs_18_.1), custom_call_target="tpu_custom_call" | custom-call | flops 1207959552 | bytes 7864320 | tf_op jit(solution)/shard_map/out_norm/pallas_call | solution.py:233
  181.6 4.5 broadcast_select_fusion.1
  186.2 2.7 maximum_dynamic-update-slice_fusion.gate_weight.up_weight
  188.9 34.8 %feed_forward.1 = (f32[1024,3072]{1,0:T(8,128)}, f32[1024,3072]{1,0:T(8,128)}, bf16[1024,768]{1,0:T(8,128)(2,1)}, f32[1024,768]{1,0:T(8,128)}, bf16[1024,768]{1,0:T(8,128)(2,1)}, /*index=5*/f32[2,768]{1,0:T(2,128)}) custom-call(bf16[1024,768]{1,0:T(8,128)(2,1)} %get-tuple-element.53.hidden_low, ...), custom_call_target="tpu_custom_call" | custom-call | flops 14495514624 | bytes 25165824 | tf_op jit(solution)/shard_map/feed_forward/pallas_call | solution.py:319
  223.7 50.3 %feed_backward.1 = (bf16[768,3072]{1,0:T(8,128)(2,1)}, bf16[768,3072]{1,0:T(8,128)(2,1)}, bf16[3072,768]{1,0:T(8,128)(2,1)}, f32[1024,768]{1,0:T(8,128)}, bf16[1024,768]{1,0:T(8,128)(2,1)}, /*index=5*/f32[2,768]{1,0:T(2,128)}) custom-call(bf16[1024,768]{1,0:T(8,128)(2,1)} %get-tuple-element.56.grad_low, bf16[1024,768]{1,0:T(8,128)(2,1)} %get-tuple-element.53.hidden_low, ...), custom_call_target="tpu_custom_call" | custom-call | flops 28991029248 | bytes 25165824 | tf_op jit(solution)/shard_map/feed_backward/pallas_call | solution.py:464
  274.0 4.1 convolution_convert_fusion.1.grad_mixed
  278.1 2.4 convolution_convert_fusion.2.refs_3_
  280.6 27.4 %attend_backward.1 = (bf16[768,1024]{1,0:T(8,128)(2,1)}, bf16[768,1024]{1,0:T(8,128)(2,1)}, bf16[768,1024]{1,0:T(8,128)(2,1)}) custom-call(bf16[2304,1024]{1,0:T(8,128)(2,1)} %qkv_rope.1.queries.key_rows.value_rows, bf16[2304,1024]{1,0:T(8,128)(2,1)} %qkv_rope.1.queries.key_rows.value_rows, bf16[2304,1024]{1,0:T(8,128)(2,1)} %qkv_rope.1.queries.key_rows.value_rows, ...), custom_call_target="tpu_custom_call" | custom-call | flops 25769803776 | bytes 25165824 | tf_op jit(solution)/shard_map/attend_backward/pallas_call | solution.py:181
  311.6 5.3 fusion.refs_4_
  317.0 7.3 %add_convert_fusion = bf16[1024,768]{1,0:T(8,128)(2,1)} fusion(f32[1024,768]{1,0:T(8,128)S(1)} %copy-done.22, bf16[2304,1024]{1,0:T(8,128)(2,1)S(1)} %constant_dynamic-update-slice_fusion, bf16[768,2304]{1,0:T(8,128)(2,1)} %maximum_dynamic-update-slice_fusion.2.weight), kind=kOutput, calls=%fused_computation.3 | convolution fusion | flops 3625451520 | bytes 12976128 | tf_op jit(solution)/shard_map/dot_general | solution.py:30
  324.9 235.2 %finish.1 = (bf16[768,6144]{1,0:T(8,128)(2,1)}, f32[384,6144]{1,0:T(8,128)}, f32[384,6144]{1,0:T(8,128)}, bf16[3072,768]{1,0:T(8,128)(2,1)}, f32[1536,768]{1,0:T...) custom-call(bf16[768,3072]{1,0:T(8,128)(2,1)} %get-tuple-element.67., ...), custom_call_target="tpu_custom_call" | custom-call | tf_op jit(solution)/shard_map/finish/pallas_call | solution.py:654
  560.1 4.1 copy.63
  565.3 8.6 %copy.65 = bf16[768,6144]{1,0:T(8,128)(2,1)} copy(bf16[768,6144]{1,0:T(8,128)(2,1)} %get-tuple-element.128) | data formatting | bytes 18874368
  573.9 5.2 copy.66
  579.1 1.8 copy.67
  580.9 1.8 copy.68
  587.4 4.8 copy.71
  594.0 3.7 copy.72
  597.8 4.8 copy.73
  602.6 4.9 copy.74
  (107 shorter events, 34.1 us)
Async XLA Ops:
  6.3 68.9 %collective-permute-start = (bf16[192,2304]{1,0:T(8,128)(2,1)}, bf16[192,2304]{1,0:T(8,128)(2,1)}, u32[]{:S(2)}, u32[]{:S(2)}) collective-permute-start(bf16[192,2304]{1,0:T(8,128)(2,1)} %constant_dynamic-slice_fusion.3), channel_id=1, source_target_pairs={{0,1},{1,0},{2,3},{3,2},{4,5},{5,4},{6,7},{7,6},{8,9},{9,8},{10,11... | collective-permute-start | bytes 2654216 | tf_op jit(solution)/shard_map/ppermute | solution.py:509
  15.2 58.4 %collective-permute-start.7 = (bf16[384,768]{1,0:T(8,128)(2,1)}, bf16[384,768]{1,0:T(8,128)(2,1)}, u32[]{:S(2)}, u32[]{:S(2)}) collective-permute-start(bf16[384,768]{1,0:T(8,128)(2,1)} %constant_dynamic-slice_fusion), channel_id=1, source_target_pairs={{0,1},{1,0},{2,3},{3,2},{4,5},{5,4},{6,7},{7,6},{8,9},{9,8},{10,11... | collective-permute-start | bytes 1769480 | tf_op jit(solution)/shard_map/ppermute | solution.py:509
  27.0 49.6 %collective-permute-start.4 = (bf16[96,6144]{1,0:T(8,128)(2,1)S(1)}, bf16[96,6144]{1,0:T(8,128)(2,1)S(1)}, u32[]{:S(2)}, u32[]{:S(2)}) collective-permute-start(bf16[96,6144]{1,0:T(8,128)(2,1)S(1)} %constant_dynamic-slice_fusion.1), channel_id=1, source_target_pairs={{0,1},{1,0},{2,3},{3,2},{4,5},{5,4},{6,7},{7,6},{8,9},{9,8},{10,11... | collective-permute-start | bytes 3538952 | tf_op jit(solution)/shard_map/ppermute | solution.py:509
  29.4 44.1 %collective-permute-start.2 = (bf16[192,768]{1,0:T(8,128)(2,1)S(1)}, bf16[192,768]{1,0:T(8,128)(2,1)}, u32[]{:S(2)}, u32[]{:S(2)}) collective-permute-start(bf16[192,768]{1,0:T(8,128)(2,1)S(1)} %constant_dynamic-slice_fusion.2), channel_id=1, source_target_pairs={{0,1},{1,0},{2,3},{3,2},{4,5},{5,4},{6,7},{7,6},{8,9},{9,8},{10,11... | collective-permute-start | bytes 884744 | tf_op jit(solution)/shard_map/ppermute | solution.py:509
  73.5 2.0 collective-permute-start.3
  73.5 16.4 %collective-permute-start.8 = (bf16[384,768]{1,0:T(8,128)(2,1)}, bf16[384,768]{1,0:T(8,128)(2,1)}, u32[]{:S(2)}, u32[]{:S(2)}) collective-permute-start(bf16[384,768]{1,0:T(8,128)(2,1)} %collective-permute-done.7), channel_id=1, source_target_pairs={{0,4},{2,6},{4,0},{6,2},{8,12},{10,14},{12,8},{14,10},{16,20},{18,... | collective-permute-start | bytes 1769480 | tf_op jit(solution)/shard_map/ppermute | solution.py:509
  75.2 17.1 %collective-permute-start.1 = (bf16[192,2304]{1,0:T(8,128)(2,1)}, bf16[192,2304]{1,0:T(8,128)(2,1)}, u32[]{:S(2)}, u32[]{:S(2)}) collective-permute-start(bf16[192,2304]{1,0:T(8,128)(2,1)} %collective-permute-done), channel_id=1, source_target_pairs={{0,2},{2,0},{4,6},{6,4},{8,10},{10,8},{12,14},{14,12},{16,18},{18,... | collective-permute-start | bytes 2654216 | tf_op jit(solution)/shard_map/ppermute | solution.py:509
  76.6 15.8 %copy-start.12 = (bf16[768,768]{1,0:T(8,128)(2,1)}, bf16[768,768]{1,0:T(8,128)(2,1)S(1)}, u32[]{:S(2)}) copy-start(bf16[768,768]{1,0:T(8,128)(2,1)S(1)} %maximum_dynamic-update-slice_fusion.3.weight) | copy-start | bytes 3538948
  76.6 38.1 %collective-permute-start.5 = (bf16[96,6144]{1,0:T(8,128)(2,1)S(1)}, bf16[96,6144]{1,0:T(8,128)(2,1)S(1)}, u32[]{:S(2)}, u32[]{:S(2)}) collective-permute-start(bf16[96,6144]{1,0:T(8,128)(2,1)S(1)} %collective-permute-done.4), channel_id=1, source_target_pairs={{0,4},{2,6},{4,0},{6,2},{8,12},{10,14},{12,8},{14,10},{16,20},{18,... | collective-permute-start | bytes 3538952 | tf_op jit(solution)/shard_map/ppermute | solution.py:509
  92.4 87.2 %collective-permute-start.9 = (bf16[768,768]{1,0:T(8,128)(2,1)}, bf16[768,768]{1,0:T(8,128)(2,1)}, u32[]{:S(2)}, u32[]{:S(2)}) collective-permute-start(bf16[768,768]{1,0:T(8,128)(2,1)} %pad_maximum_fusion.1), channel_id=1, source_target_pairs={{0,2},{2,0},{4,6},{6,4},{8,10},{10,8},{12,14},{14,12},{16,18},{18,... | collective-permute-start | bytes 3538952 | tf_op jit(solution)/shard_map/ppermute | solution.py:509
  116.5 65.1 %collective-permute-start.6 = (bf16[192,6144]{1,0:T(8,128)(2,1)}, bf16[192,6144]{1,0:T(8,128)(2,1)}, u32[]{:S(2)}, u32[]{:S(2)}) collective-permute-start(bf16[192,6144]{1,0:T(8,128)(2,1)} %pad_maximum_fusion), channel_id=1, source_target_pairs={{0,2},{2,0},{4,6},{6,4},{8,10},{10,8},{12,14},{14,12},{16,18},{18,... | collective-permute-start | bytes 7077896 | tf_op jit(solution)/shard_map/ppermute | solution.py:509
  117.9 63.5 %slice-start.6 = ((s8[4718592]{0:T(1024)(128)(4,1)}), s8[4194304]{0:T(1024)(128)(4,1)S(1)}, s32[]{:S(2)}) async-start(s8[4718592]{0:T(1024)(128)(4,1)} %bitcast.14), calls=%async_computation.6 | async-start | bytes 8388608
  128.8 52.5 %slice-start.7 = ((s8[4718592]{0:T(1024)(128)(4,1)}), s8[524288]{0:T(1024)(128)(4,1)S(1)}, s32[]{:S(2)}) async-start(s8[4718592]{0:T(1024)(128)(4,1)} %bitcast.14), calls=%async_computation.7 | async-start | bytes 1048576
  181.6 7.3 %copy-start.3 = (bf16[3072,768]{1,0:T(8,128)(2,1)}, bf16[3072,768]{1,0:T(8,128)(2,1)S(1)}, u32[]{:S(2)}) copy-start(bf16[3072,768]{1,0:T(8,128)(2,1)S(1)} %maximum_dynamic-update-slice_fusion.1.down_weight) | copy-start | bytes 14155780
  223.7 50.3 %copy-start.13 = (bf16[768,768]{1,0:T(8,128)(2,1)S(1)}, bf16[768,768]{1,0:T(8,128)(2,1)}, u32[]{:S(2)}) copy-start(bf16[768,768]{1,0:T(8,128)(2,1)} %copy-done.12) | copy-start | bytes 3538948
  274.0 4.1 copy-start.20
  274.0 4.1 copy-start.21
  311.6 5.3 copy-start.22
  317.0 7.3 %copy-start.17 = (f32[2,768]{1,0:T(2,128)S(1)}, f32[2,768]{1,0:T(2,128)}, u32[]{:S(2)}) copy-start(f32[2,768]{1,0:T(2,128)} %get-tuple-element.71) | copy-start | bytes 18436
  317.0 7.3 %copy-start.18 = (f32[2,768]{1,0:T(2,128)S(1)}, f32[2,768]{1,0:T(2,128)}, u32[]{:S(2)}) copy-start(f32[2,768]{1,0:T(2,128)} %get-tuple-element.70) | copy-start | bytes 18436
  560.1 4.1 copy-start.11
  573.9 5.2 copy-start.6
  573.9 7.0 %copy-start.5 = (f32[384,2304]{1,0:T(8,128)S(1)}, f32[384,2304]{1,0:T(8,128)}, u32[]{:S(2)}) copy-start(f32[384,2304]{1,0:T(8,128)} %get-tuple-element.131) | copy-start | bytes 10616836
  579.1 8.3 %slice-start.3 = ((s8[9437184]{0:T(1024)(128)(4,1)}), s8[4194304]{0:T(1024)(128)(4,1)S(1)}, s32[]{:S(2)}) async-start(s8[9437184]{0:T(1024)(128)(4,1)} %bitcast.12), calls=%async_computation.3 | async-start | bytes 8388608
  579.1 8.3 %slice-start.4 = ((s8[9437184]{0:T(1024)(128)(4,1)}), s8[4194304]{0:T(1024)(128)(4,1)S(1)}, s32[]{:S(2)}) async-start(s8[9437184]{0:T(1024)(128)(4,1)} %bitcast.12), calls=%async_computation.4 | async-start | bytes 8388608
  580.9 6.5 %slice-start.5 = ((s8[9437184]{0:T(1024)(128)(4,1)}), s8[1048576]{0:T(1024)(128)(4,1)S(1)}, s32[]{:S(2)}) async-start(s8[9437184]{0:T(1024)(128)(4,1)} %bitcast.12), calls=%async_computation.5 | async-start | bytes 2097152
  586.4 5.8 slice-start
  587.4 6.4 %slice-start.1 = ((s8[9437184]{0:T(1024)(128)(4,1)}), s8[4194304]{0:T(1024)(128)(4,1)S(1)}, s32[]{:S(2)}) async-start(s8[9437184]{0:T(1024)(128)(4,1)} %bitcast.10), calls=%async_computation.1 | async-start | bytes 8388608
  587.4 6.6 %slice-start.2 = ((s8[9437184]{0:T(1024)(128)(4,1)}), s8[1048576]{0:T(1024)(128)(4,1)S(1)}, s32[]{:S(2)}) async-start(s8[9437184]{0:T(1024)(128)(4,1)} %bitcast.10), calls=%async_computation.2 | async-start | bytes 2097152
  602.6 4.9 copy-start.16
  602.6 5.5 copy-start.15
  602.6 6.1 copy-start.14
  (9 other events, 20.7 us)
